TPU v7x, 256 devices: a whole 4x4x8 slice. The times are simulated.
256 devices in a mesh: dp: 256 (over z, y, x, core).
Axes of the slice: x: 4, y: 4, z: 8, core: 2. Of those that a mesh axis runs over, the one named last changes fastest.
Arguments:
- inputs: bfloat16 [98304, 1024], P('dp'), may hold values from -8 to 8
- grad_out: bfloat16 [98304, 1024], P('dp'), may hold values from -0.019042969 to 0.019042969
- norm_gain: float32 [1024], replicated, may hold values from 0.5 to 1.5
- master: float32 [1024, 4096], P('dp'), may hold values from -0.25 to 0.25
- projector: bfloat16 [1024, 256], P('dp'), may hold values from -0.1875 to 0.1875
- moment_first: float32 [256, 4096], P('dp'), may hold values from -0.6 to 0.6
- moment_second: float32 [256, 4096], P('dp'), may hold values from 0.001 to 0.01
- doc_lengths: int32 [256, 4], P('dp'), may hold values from 1 to 192, 384 in all within a row
Outputs:
- new_master: float32 [1024, 4096], P('dp')
- new_first: float32 [256, 4096], P('dp')
- new_second: float32 [256, 4096], P('dp')
All inputs are finite; a program needn't handle non-finite values.
Results may differ from a plain program's by a relative error of at most 0.0025.
Values may be sent and summed in bfloat16 or wider, within the bound.
A program may use at most 128 MiB of HBM per device.

v0:
```python
import jax
import jax.numpy as jnp
from jax import lax
from jax.sharding import PartitionSpec as P

DH = 64


beta_one = 0.9
beta_two = 0.999
adam_eps = 1e-08
adam_step = 10.0
learn_rate = 0.01
galore_scale = 0.25
norm_eps = 1e-05


def doc_mask(lengths_row, count):
    position = jnp.arange(count, dtype=jnp.int32)
    bounds = jnp.cumsum(lengths_row)
    segment = jnp.sum((position[:, None] >= bounds[None, :]).astype(jnp.int32), axis=1)
    return (segment[:, None] == segment[None, :]) & (position[:, None] >= position[None, :])


def attend(queries, key_rows, value_rows, grad_head, visible):
    highest = lax.Precision.HIGHEST
    factor = queries.shape[1] ** (-0.5)
    scores = jnp.dot(queries, key_rows.T, preferred_element_type=jnp.float32) * factor
    scores = jnp.where(visible, scores, jnp.float32(-1e30))
    row_max = jnp.max(scores, axis=1, keepdims=True)
    lifted = jnp.exp(scores - row_max)
    probs = lifted / jnp.sum(lifted, axis=1, keepdims=True)
    attended = jnp.dot(
        probs.astype(jnp.bfloat16), value_rows, preferred_element_type=jnp.float32
    ).astype(jnp.bfloat16)
    grad_values = jnp.dot(probs.T, grad_head, precision=highest)
    grad_probs = jnp.dot(grad_head, value_rows.astype(jnp.float32).T, precision=highest)
    grad_scores = probs * (grad_probs - jnp.sum(probs * grad_probs, axis=1, keepdims=True))
    grad_queries = jnp.dot(grad_scores, key_rows.astype(jnp.float32), precision=highest) * factor
    grad_keys = jnp.dot(grad_scores.T, queries.astype(jnp.float32), precision=highest) * factor
    return (attended, grad_queries, grad_keys, grad_values)


def attend_heads(projected, grad_head, lengths_row, head_size):
    count = projected.shape[0]
    width = grad_head.shape[1]
    heads = width // head_size
    visible = doc_mask(lengths_row, count)
    queries = projected[:, :width].reshape(count, heads, head_size)
    key_rows = projected[:, width : 2 * width].reshape(count, heads, head_size)
    value_rows = projected[:, 2 * width :].reshape(count, heads, head_size)
    grad_rows = grad_head.reshape(count, heads, head_size)
    per_head = jax.vmap(attend, in_axes=(1, 1, 1, 1, None), out_axes=1)
    attended, grad_queries, grad_keys, grad_values = per_head(
        queries, key_rows, value_rows, grad_rows, visible
    )
    grad_projected = jnp.concatenate(
        [
            grad_queries.reshape(count, width),
            grad_keys.reshape(count, width),
            grad_values.reshape(count, width),
        ],
        axis=1,
    ).astype(jnp.bfloat16)
    return (attended.reshape(count, width), grad_projected)


def normalize(inputs, norm_gain):
    values = inputs.astype(jnp.float32)
    scale = lax.rsqrt(jnp.mean(values * values, axis=1, keepdims=True) + norm_eps)
    return (values * scale * norm_gain[None, :]).astype(jnp.bfloat16)


def shards(
    inputs, grad_out, norm_gain, master, projector, moment_first, moment_second, doc_lengths
):
    highest = lax.Precision.HIGHEST
    width = master.shape[1] // 4
    contract = (((0,), (0,)), ((), ()))
    gathered = lax.all_gather(master.astype(jnp.bfloat16), "dp", axis=0, tiled=True)
    normed = normalize(inputs, norm_gain)
    projected = jnp.dot(
        normed, gathered[:, : 3 * width], preferred_element_type=jnp.float32
    ).astype(jnp.bfloat16)
    grad_head = jnp.dot(grad_out, gathered[:, 3 * width :], preferred_element_type=jnp.float32)
    attended, grad_projected = attend_heads(projected, grad_head, doc_lengths[0], DH)
    projector_own = projector.astype(jnp.float32)
    grad_inner = lax.dot_general(
        normed, grad_projected, contract, preferred_element_type=jnp.float32
    )
    grad_outer = lax.dot_general(grad_out, attended, contract, preferred_element_type=jnp.float32)
    grads = jnp.concatenate([grad_inner, grad_outer], axis=1)
    owned = lax.psum_scatter(grads, "dp", scatter_dimension=0, tiled=True)
    term = lax.dot_general(projector_own, owned, contract, precision=highest)
    low_own = lax.psum_scatter(term, "dp", scatter_dimension=0, tiled=True)
    new_first = beta_one * moment_first + (1.0 - beta_one) * low_own
    new_second = beta_two * moment_second + (1.0 - beta_two) * low_own * low_own
    direction = (
        new_first
        / (1.0 - beta_one**adam_step)
        / (jnp.sqrt(new_second / (1.0 - beta_two**adam_step)) + adam_eps)
    )
    direction_full = lax.all_gather(direction, "dp", axis=0, tiled=True)
    new_master = master - learn_rate * galore_scale * jnp.dot(
        projector_own, direction_full, precision=highest
    )
    return (new_master, new_first, new_second)


def solution(mesh):
    return jax.shard_map(
        shards,
        mesh=mesh,
        in_specs=(
            P("dp", None),
            P("dp", None),
            P(),
            P("dp", None),
            P("dp", None),
            P("dp", None),
            P("dp", None),
            P("dp", None),
        ),
        out_specs=(P("dp", None), P("dp", None), P("dp", None)),
        check_vma=False,
    )
```

profile of v0, /device:TPU:1, one launch (start us, length us, event | category | flops | bytes accessed | tf_op | source)
XLA Modules:
  0.0 931.6 jit_solution(8602638055454135452)
XLA Ops:
  7.2 0.0 copy-start
  7.2 0.0 copy-start.2
  7.2 0.0 copy-start.6
  7.2 0.0 all-gather.5.cloned.1.call-start
  7.2 1.6 convert_bitcast_fusion
  8.8 0.0 all-gather.5.cloned.1.call-update
  8.8 0.0 all-reduce.5.cloned.1.call-start
  8.9 0.8 reduce-window.8
  9.7 0.1 convert_reduce_fusion
  9.8 1.4 fusion.24
  11.2 0.1 fusion.30
  11.3 123.3 %all-gather.5.cloned.1.call-done = bf16[256,4,4096]{2,1,0:T(4,128)(2,1)} async-done(((bf16[1,4,4096]{2,1,0:T(4,128)(2,1)}), bf16[256,4,4096]{2,1,0:T(4,128)(2,1)}) %all-gather.5.cloned.1.call-update) | async-done | bytes 8388624 | tf_op jit(solution)/shard_map/all_gather | solution.py:80
  134.6 12.5 %reshape.82 = bf16[1024,4096]{1,0:T(8,128)(2,1)} reshape(bf16[256,4,4096]{2,1,0:T(4,128)(2,1)} %all-gather.5.cloned.1.call-done) | data formatting | bytes 16777216
  147.2 0.0 copy-done.2
  147.2 0.0 copy-done.6
  147.2 5.5 fusion.9
  152.6 1.4 fusion.43
  154.1 0.4 copy.73
  154.4 1.5 copy.74
  155.9 2.3 copy.76
  158.3 0.0 copy-done
  158.3 2.9 fusion.22
  161.2 1.6 fusion
  162.7 0.0 copy-start.1
  162.7 1.9 fusion.2
  164.7 0.0 copy-start.5
  164.7 13.4 %convolution_convert_fusion = bf16[16,384,64]{1,2,0:T(8,128)(2,1)} fusion(f32[384,16,64]{0,2,1:T(8,128)S(1)} %bitcast.64, f32[16,384,384]{1,2,0:T(8,128)S(1)} %get-tuple-element.22, f32[16,384]{1,0:T(8,128)S(1)} %fusion.2, f32[16,384]{1,0:T(8,128)S(1)} %get-tuple-element.21, pred[384,384]{0,1:T(8,128)(4,1)S(1)} %fusion.30), kind=kOutput, calls=%fused_computation.38 | convolution fusion | flops 1821769728 | bytes 11993088 | tf_op jit(solution)/shard_map/vmap()/dot_general | solution.py:36
  178.1 0.0 copy-done.1
  178.1 0.0 copy-done.5
  178.1 9.1 multiply_reduce_fusion
  187.2 15.6 %multiply_convert_fusion = bf16[16,384,64]{1,2,0:T(8,128)(2,1)} fusion(bf16[384,16,64]{0,2,1:T(8,128)(2,1)S(1)} %bitcast.53, f32[16,384,384]{1,2,0:T(8,128)} %get-tuple-element.24, f32[16,384]{1,0:T(8,128)S(1)} %get-tuple-element.23, f32[16,384,384]{1,2,0:T(8,128)} %copy-done.1, f32[16,384]{1,0:T(8,128)S(1)} %fusion.2, ...), kind=kOutput, calls=%fused_computation.35 | convolution fusion | flops 1826881536 | bytes 20668416 | tf_op jit(solution)/shard_map/vmap()/dot_general | solution.py:40
  202.8 13.0 %multiply_convert_fusion.1 = bf16[16,384,64]{1,2,0:T(8,128)(2,1)S(1)} fusion(bf16[384,16,64]{0,2,1:T(8,128)(2,1)S(1)} %bitcast.55, f32[16,384,384]{1,2,0:T(8,128)} %get-tuple-element.24, f32[16,384]{1,0:T(8,128)S(1)} %get-tuple-element.23, f32[16,384,384]{1,2,0:T(8,128)} %copy-done.1, f32[16,384]{1,0:T(8,128)S(1)} %fusion.2, ...), kind=kOutput, calls=%fused_computation.36 | convolution fusion | flops 1826881536 | bytes 20668416 | tf_op jit(solution)/shard_map/vmap()/dot_general | solution.py:39
  215.8 6.8 fusion.27
  222.6 0.0 copy-start.3
  222.6 0.0 copy-start.4
  222.6 1.3 convolution_bitcast_fusion.1
  223.9 0.0 copy-done.3
  224.0 0.0 copy-done.4
  224.0 3.7 fusion.16
  227.7 6.0 pad_maximum_fusion
  233.7 0.0 copy-start.10
  233.7 0.0 all-reduce.5.cloned.1.call-update
  233.7 0.0 copy-start.8
  233.7 0.0 copy-start.9
  233.7 0.0 copy-start.7
  233.7 0.0 all-reduce.7.cloned.1.call-start
  233.8 292.1 %all-reduce.5.cloned.1.call-done = f32[1024,4096]{1,0:T(8,128)} async-done(((f32[1024,4096]{1,0:T(8,128)}), f32[1024,4096]{1,0:T(8,128)}) %all-reduce.5.cloned.1.call-update) | async-done | bytes 16777232
  525.9 0.0 copy-done.10
  525.9 4.7 convolution_bitcast_fusion
  530.6 0.0 all-reduce.7.cloned.1.call-update
  530.7 0.2 all-gather.7.cloned.1.call-start
  530.9 267.7 %all-reduce.7.cloned.1.call-done = f32[256,4096]{0,1:T(8,128)} async-done(((f32[256,4096]{0,1:T(8,128)}), f32[256,4096]{0,1:T(8,128)}) %all-reduce.7.cloned.1.call-update) | async-done | bytes 4194320
  798.6 2.2 constant_dynamic-slice_fusion
  800.8 0.6 copy.82
  801.4 0.0 copy-done.8
  801.4 0.0 copy-done.9
  801.4 0.7 fusion.35
  802.1 0.0 all-gather.7.cloned.1.call-update
  802.2 116.3 %all-gather.7.cloned.1.call-done = f32[256,1,4096]{2,1,0:T(1,128)} async-done(((f32[1,1,4096]{2,1,0:T(1,128)}), f32[256,1,4096]{2,1,0:T(1,128)}) %all-gather.7.cloned.1.call-update) | async-done | bytes 4194320 | tf_op jit(solution)/shard_map/all_gather | solution.py:103
  918.5 0.0 copy-done.7
  918.5 6.4 fusion.8
  (1 shorter events, 0.0 us)
Async XLA Ops:
  7.2 151.1 %copy-start = (bf16[384,1024]{1,0:T(8,128)(2,1)S(1)}, bf16[384,1024]{1,0:T(8,128)(2,1)}, u32[]{:S(2)}) copy-start(bf16[384,1024]{1,0:T(8,128)(2,1)} %param.9) | copy-start | bytes 2359300
  7.2 140.0 %copy-start.2 = (bf16[384,1024]{1,0:T(8,128)(2,1)S(1)}, bf16[384,1024]{1,0:T(8,128)(2,1)}, u32[]{:S(2)}) copy-start(bf16[384,1024]{1,0:T(8,128)(2,1)} %param.8) | copy-start | bytes 2359300
  7.2 140.0 %copy-start.6 = (f32[1024]{0:T(1024)S(1)}, f32[1024]{0:T(1024)}, u32[]{:S(2)}) copy-start(f32[1024]{0:T(1024)} %param.10) | copy-start | bytes 12292
  7.2 127.4 %all-gather.5.cloned.1.call-start = ((), (), s32[]{:S(2)}) async-start(), calls=%async_computation | async-start | bytes 8421376 | tf_op jit(solution)/shard_map/all_gather | solution.py:80
  8.8 517.1 %all-reduce.5.cloned.1.call-start = ((), (), s32[]{:S(2)}) async-start(), calls=%async_computation.2 | async-start | bytes 33554432
  162.7 15.4 %copy-start.1 = (f32[16,384,384]{1,2,0:T(8,128)}, f32[16,384,384]{1,2,0:T(8,128)S(1)}, u32[]{:S(2)}) copy-start(f32[16,384,384]{1,2,0:T(8,128)S(1)} %get-tuple-element.22) | copy-start | bytes 28311556
  164.7 13.4 %copy-start.5 = (bf16[384,1024]{0,1:T(8,128)(2,1)S(1)}, bf16[384,1024]{0,1:T(8,128)(2,1)}, u32[]{:S(2)}) copy-start(bf16[384,1024]{0,1:T(8,128)(2,1)} %copy.76) | copy-start | bytes 2359300
  222.6 1.3 copy-start.3
  222.6 1.4 copy-start.4
  233.7 292.2 %copy-start.10 = (bf16[4,256]{1,0:T(4,128)(2,1)S(1)}, bf16[4,256]{1,0:T(4,128)(2,1)}, u32[]{:S(2)}) copy-start(bf16[4,256]{1,0:T(4,128)(2,1)} %param.12) | copy-start | bytes 6148
  233.7 567.7 %copy-start.8 = (f32[1,4096]{1,0:T(1,128)S(1)}, f32[1,4096]{1,0:T(1,128)}, u32[]{:S(2)}) copy-start(f32[1,4096]{1,0:T(1,128)} %param.13) | copy-start | bytes 49156
  233.7 567.7 %copy-start.9 = (f32[1,4096]{1,0:T(1,128)S(1)}, f32[1,4096]{1,0:T(1,128)}, u32[]{:S(2)}) copy-start(f32[1,4096]{1,0:T(1,128)} %param.14) | copy-start | bytes 49156
  233.7 684.8 %copy-start.7 = (f32[4,4096]{1,0:T(4,128)S(1)}, f32[4,4096]{1,0:T(4,128)}, u32[]{:S(2)}) copy-start(f32[4,4096]{1,0:T(4,128)} %param.11) | copy-start | bytes 196612
  233.7 564.9 %all-reduce.7.cloned.1.call-start = ((), (), s32[]{:S(2)}) async-start(), calls=%async_computation.3 | async-start | bytes 8388608
  530.7 387.8 %all-gather.7.cloned.1.call-start = ((), (), s32[]{:S(2)}) async-start(), calls=%async_computation.1 | async-start | bytes 4210688 | tf_op jit(solution)/shard_map/all_gather | solution.py:103
Sparse Core Ops, SparseCore 0:
  12.2 122.4 all-gather.4
  233.8 292.0 all-reduce.4
  532.3 266.2 all-reduce.6
  802.6 115.8 all-gather.6
where the time goes:
time: 941 us; the launch traced here: 932 us
  waiting for transfers between devices  800 us (85%)
  matrix products  83.9 us (9%)
  local copies, waits for them, and re-layouts  21 us (2%)
  between operations  14.1 us (1%)
  other arithmetic  12.7 us (1%)
    unnamed x6, waiting for transfers between devices  560 us
    all_gather x1, waiting for transfers between devices, shards(): lax.all_gather(master.astype(jnp.bfloat16), 'dp', axis=0, tiled=True)  123 us
    all_gather x1, waiting for transfers between devices, shards(): direction_full = lax.all_gather(direction, 'dp', axis=0, tiled=True)  116 us
  transfers between devices with their start and end apart: 4, of which 4 were waited for; matrix products, arithmetic and copies ran while one was open for 0% of the time, Pallas kernels for 0%

commit v1 on v0

v1 whole, which is shorter than its diff:
```python
import jax
import jax.numpy as jnp
import numpy as np
from jax import lax
from jax.experimental import pallas as pl
from jax.experimental.pallas import tpu as pltpu
from jax.sharding import PartitionSpec as P

NZ, NY, NX, NC = 8, 4, 4, 2
SIZE = {"z": NZ, "y": NY, "x": NX}
TOK = 384
WIDTH = 1024
RANK = 256
PART = 384
VMEM_LIMIT = 56 * 1024 * 1024

beta_one = 0.9
beta_two = 0.999
adam_eps = 1e-08
adam_step = 10.0
learn_rate = 0.01
galore_scale = 0.25
norm_eps = 1e-05

F32 = jnp.float32
BF16 = jnp.bfloat16
MESH = pl.DeviceIdType.MESH


def place():
    me = lax.axis_index("dp")
    c = lax.rem(me, NC)
    x = lax.rem(me // NC, NX)
    y = lax.rem(me // (NC * NX), NY)
    z = me // (NC * NX * NY)
    return {"z": z, "y": y, "x": x, "c": c}


def device_at(where, **moved):
    at = dict(where, **moved)
    return ((at["z"] * NY + at["y"]) * NX + at["x"]) * NC + at["c"]


def shifted(where, axis, by):
    n = SIZE[axis]
    return lax.rem(where[axis] + (by + n), n)


class Sender:
    def __init__(self, send_sems, recv_sems):
        self.send_sems, self.recv_sems = send_sems, recv_sems
        self.copies = []

    def send(self, src, dst, device):
        i = len(self.copies)
        copy = pltpu.make_async_remote_copy(
            src_ref=src,
            dst_ref=dst,
            send_sem=self.send_sems.at[i],
            recv_sem=self.recv_sems.at[i],
            device_id=(device,),
            device_id_type=MESH,
        )
        copy.start()
        self.copies.append(copy)
        return copy

    def finish(self):
        for copy in self.copies:
            copy.wait_send()


def greet(devices):
    barrier = pltpu.get_barrier_semaphore()
    for device in devices:
        pl.semaphore_signal(barrier, inc=1, device_id=(device,), device_id_type=MESH)
    pl.semaphore_wait(barrier, len(devices))


def run_together(steps):
    live = list(steps)
    while live:
        still = []
        for step in live:
            try:
                next(step)
                still.append(step)
            except StopIteration:
                pass
        live = still


ORDERS = (("x", "y", "z"), ("y", "z", "x"), ("z", "x", "y"))


def gather_part(part, order, where, sender, piece, w_ref, local_sem, from_sibling):
    c = where["c"]
    sibling = device_at(where, c=1 - c)

    def chunk(stage, value, half=None, core=c):
        index = {}
        for i, axis in enumerate(order):
            if i < stage:
                index[axis] = slice(None)
            elif i == stage:
                index[axis] = value
            else:
                index[axis] = where[axis]
        if half is not None:
            n = SIZE[order[0]] // 2
            index[order[0]] = pl.ds(half * n, n)
        return w_ref.at[part, core, index["z"], index["y"], index["x"]]

    own = w_ref.at[part, c, where["z"], where["y"], where["x"]]
    local = pltpu.make_async_copy(piece.at[part], own, local_sem)
    local.start()
    for stage in range(3):
        axis = order[stage]
        n = SIZE[axis]
        right = device_at(where, **{axis: shifted(where, axis, 1)})
        left = device_at(where, **{axis: shifted(where, axis, -1)})
        last = stage == 2

        def pass_on(ref):
            if last:
                from_sibling.append(sender.send(ref, ref, sibling))

        start = chunk(stage, where[axis])
        src = piece.at[part] if stage == 0 else start
        to_right = sender.send(src, start, right)
        to_left = sender.send(src, start, left)
        pass_on(start)
        for step in range(1, n // 2):
            yield
            end = step == n // 2 - 1
            behind = shifted(where, axis, -step)
            ahead = shifted(where, axis, step)
            to_right.wait_recv()
            got = chunk(stage, behind)
            if not end:
                to_right = sender.send(got, got, right)
            elif stage == 0:
                to_right = sender.send(got, got, right)
            else:
                ref = chunk(stage, behind, 0)
                to_right = sender.send(ref, ref, right)
            pass_on(got)
            to_left.wait_recv()
            got = chunk(stage, ahead)
            if not end:
                to_left = sender.send(got, got, left)
            elif stage == 0:
                to_left = None
            else:
                ref = chunk(stage, ahead, 1)
                to_left = sender.send(ref, ref, left)
            pass_on(got)
        yield
        to_right.wait_recv()
        if to_left is not None:
            to_left.wait_recv()
        pass_on(chunk(stage, shifted(where, axis, n // 2)))
        if stage == 0:
            local.wait()


def weights_kernel(
    master_ref, proj_ref, w_ref, quad_w, quad_p, own_p, rows_w, rows_p, piece,
    local_sems, send_sems, recv_sems
):
    where = place()
    c, x = where["c"], where["x"]
    flip = x + 1 - 2 * lax.rem(x, 2)
    neighbours = [device_at(where, c=1 - c), device_at(where, x=flip, c=1 - c)]
    for axis in "xyz":
        for by in (1, -1):
            neighbours.append(device_at(where, **{axis: shifted(where, axis, by)}))
    greet(neighbours)
    sender = Sender(send_sems, recv_sems)
    own_p[...] = proj_ref[...].astype(F32)
    mine = lax.rem(x, 2) * 2 + c
    quad = []
    for dx, dc in ((0, 1), (1, 0), (1, 1)):
        to_x = flip if dx else x
        to_c = 1 - c if dc else c
        other = lax.rem(to_x, 2) * 2 + to_c
        to = device_at(where, x=to_x, c=to_c)
        columns = pl.ds(pl.multiple_of(other * WIDTH, WIDTH), WIDTH)
        quad.append(sender.send(master_ref.at[:, columns], quad_w.at[mine], to))
        quad.append(sender.send(own_p, quad_p.at[mine], to))
    columns = pl.ds(pl.multiple_of(mine * WIDTH, WIDTH), WIDTH)
    quad_w[mine] = master_ref[:, columns]
    quad_p[mine] = own_p[...]
    for copy in quad:
        copy.wait_recv()
    for i in range(4):
        rows_w[i * 4 : i * 4 + 4, :] = quad_w[i]
        rows_p[i * 4 : i * 4 + 4, :] = quad_p[i]
    piece[0] = rows_w[:, :PART].astype(BF16)
    piece[1] = rows_w[:, PART : 2 * PART].astype(BF16)
    piece[2, :, :256] = rows_w[:, 2 * PART :].astype(BF16)
    halves = jnp.where(c == 0, rows_p[:, :128], rows_p[:, 128:])
    piece[2, :, 256:] = halves.astype(BF16)
    from_sibling = []
    run_together(
        [
            gather_part(
                i, ORDERS[i], where, sender, piece, w_ref, local_sems.at[i], from_sibling
            )
            for i in range(3)
        ]
    )
    for copy in from_sibling:
        copy.wait_recv()
    sender.finish()


def gather_weights(master, proj):
    n_sems = 96
    return pl.pallas_call(
        weights_kernel,
        out_shape=jax.ShapeDtypeStruct((3, NC, NZ, NY, NX, 16, PART), BF16),
        in_specs=[pl.BlockSpec(memory_space=pltpu.VMEM)] * 2,
        out_specs=pl.BlockSpec(memory_space=pl.ANY),
        scratch_shapes=[
            pltpu.VMEM((4, 4, WIDTH), F32),
            pltpu.VMEM((4, 4, RANK), F32),
            pltpu.VMEM((4, RANK), F32),
            pltpu.VMEM((16, WIDTH), F32),
            pltpu.VMEM((16, RANK), F32),
            pltpu.VMEM((3, 16, PART), BF16),
            pltpu.SemaphoreType.DMA((3,)),
            pltpu.SemaphoreType.DMA((n_sems,)),
            pltpu.SemaphoreType.DMA((n_sems,)),
        ],
        compiler_params=pltpu.CompilerParams(
            collective_id=0, has_side_effects=True, vmem_limit_bytes=VMEM_LIMIT
        ),
        name="gather_weights",
    )(master, proj)


def dot(a, b, dims=((1,), (0,))):
    return lax.dot_general(a, b, (dims, ((), ())), preferred_element_type=F32)


ROWS = ((1,), (1,))
COLS = ((0,), (0,))


def split(value):
    high = value.astype(BF16)
    return high, (value - high.astype(F32)).astype(BF16)


def local_kernel(
    len_ref, in_ref, gout_ref, gain_ref, w_ref, low_ref,
    normed, q_s, k_s, v_s, gh_s, low_in, bias, np_t, gp_t
):
    values = in_ref[...].astype(F32)
    scale = lax.rsqrt(jnp.mean(values * values, axis=1, keepdims=True) + norm_eps)
    normed[...] = (values * scale * gain_ref[...]).astype(BF16)

    b0 = len_ref[0, 0]
    b1 = b0 + len_ref[0, 1]
    b2 = b1 + len_ref[0, 2]
    b3 = b2 + len_ref[0, 3]

    def segment(position):
        return sum((position >= b).astype(jnp.int32) for b in (b0, b1, b2, b3))

    row = lax.broadcasted_iota(jnp.int32, (TOK, 1), 0)
    col = lax.broadcasted_iota(jnp.int32, (1, TOK), 1)
    seen = (segment(row) == segment(col)) & (row >= col)
    bias[...] = jnp.where(seen, F32(0.0), F32(-1e30))

    def weight(part, xl, c, lo, hi):
        return w_ref[part, c, :, :, :, xl, :, lo:hi].reshape(WIDTH, hi - lo)

    def project(part, pairs):
        wide = pairs * 128
        for i in range(pairs):
            pass
        res = dot(normed[...], weight(part, 0, 0, 0, wide)).astype(BF16)
        for i in range(pairs):
            q_s[3 * part + i] = res[:, i * 128 : (i + 1) * 128]
        res = dot(normed[...], weight(part, 0, 1, 0, wide)).astype(BF16)
        for i in range(pairs):
            k_s[3 * part + i] = res[:, i * 128 : (i + 1) * 128]
        res = dot(normed[...], weight(part, 1, 0, 0, wide)).astype(BF16)
        for i in range(pairs):
            v_s[3 * part + i] = res[:, i * 128 : (i + 1) * 128]
        res = dot(gout_ref[...], weight(part, 1, 1, 0, wide))
        for i in range(pairs):
            gh_s[3 * part + i] = res[:, i * 128 : (i + 1) * 128]

    @pl.loop(0, 2)
    def _(part):
        project(part, 3)

    project(2, 2)
    for c in range(2):
        proj = weight(2, 0, c, 256, 384)
        rows = slice(c * 128, (c + 1) * 128)
        for src, out in ((normed, np_t), (gout_ref, gp_t)):
            high, rest = split(dot(src[...], proj))
            out[0, :, rows] = high
            out[1, :, rows] = rest

    lane = lax.broadcasted_iota(jnp.int32, (1, 128), 1)
    firsts = (lane < 64).astype(BF16)
    masks = (firsts, 1 - firsts)

    @pl.loop(0, 8)
    def _(pair):
        q, k, v = q_s[pair], k_s[pair], v_s[pair]
        gh_high, gh_rest = split(gh_s[pair])
        v_twice = jnp.concatenate([v, v], axis=1)
        total_q = total_k = total_v = total_a = None
        for mask in masks:
            s = dot(q * mask, k, ROWS) * 0.125 + bias[...]
            e = jnp.exp(s - jnp.max(s, axis=1, keepdims=True))
            p = e / jnp.sum(e, axis=1, keepdims=True)
            p_high, p_rest = split(p)
            a = dot(p_high, v * mask)
            gh_m = gh_high * mask
            gh_both = jnp.concatenate([gh_m, gh_rest * mask], axis=1)
            gv = dot(p_high, gh_both, COLS)
            gv = gv[:, :128] + gv[:, 128:] + dot(p_rest, gh_m, COLS)
            gp = dot(gh_both, v_twice, ROWS)
            gs = p * (gp - jnp.sum(p * gp, axis=1, keepdims=True))
            gs_high, gs_rest = split(gs)
            k_m, q_m = k * mask, q * mask
            gq = dot(gs_high, k_m) + dot(gs_rest, k_m)
            gk = dot(gs_high, q_m, COLS) + dot(gs_rest, q_m, COLS)
            if total_q is None:
                total_q, total_k, total_v, total_a = gq, gk, gv, a
            else:
                total_q, total_k = total_q + gq, total_k + gk
                total_v, total_a = total_v + gv, total_a + a
        grads = jnp.concatenate(
            [
                (total_q * 0.125).astype(BF16),
                (total_k * 0.125).astype(BF16),
                total_v.astype(BF16),
            ],
            axis=1,
        )
        low = dot(np_t[0], grads, COLS) + dot(np_t[1], grads, COLS)
        for i in range(3):
            columns = pl.ds(pl.multiple_of(i * WIDTH + pair * 128, 128), 128)
            low_ref[:, columns] = low[:, i * 128 : (i + 1) * 128]
        attended = total_a.astype(BF16)
        columns = pl.ds(pl.multiple_of(3 * WIDTH + pair * 128, 128), 128)
        low_ref[:, columns] = dot(gp_t[0], attended, COLS) + dot(gp_t[1], attended, COLS)


def local_terms(lengths, inputs, grad_out, gain, weights):
    vmem = pl.BlockSpec(memory_space=pltpu.VMEM)
    return pl.pallas_call(
        local_kernel,
        out_shape=jax.ShapeDtypeStruct((RANK, 4 * WIDTH), F32),
        in_specs=[pl.BlockSpec(memory_space=pltpu.SMEM)] + [vmem] * 4,
        out_specs=vmem,
        scratch_shapes=[
            pltpu.VMEM((TOK, WIDTH), BF16),
            pltpu.VMEM((8, TOK, 128), BF16),
            pltpu.VMEM((8, TOK, 128), BF16),
            pltpu.VMEM((8, TOK, 128), BF16),
            pltpu.VMEM((8, TOK, 128), F32),
            pltpu.VMEM((8, 128), F32),
            pltpu.VMEM((TOK, TOK), F32),
            pltpu.VMEM((2, TOK, RANK), BF16),
            pltpu.VMEM((2, TOK, RANK), BF16),
        ],
        compiler_params=pltpu.CompilerParams(vmem_limit_bytes=VMEM_LIMIT),
        name="local_terms",
    )(lengths, inputs, grad_out, gain, weights)


def update_kernel(
    low_ref, first_ref, second_ref, master_ref, prep_ref,
    new_master, new_first, new_second,
    r0, send_a, send_b, recv_a, recv_b, acc_a, acc_b, recv2_a, recv2_b,
    rows, recv3, dir_rows, tiles, lhs, send_sems, recv_sems
):
    where = place()
    c, x, y, z = where["c"], where["x"], where["y"], where["z"]
    sibling = device_at(where, c=1 - c)

    def peer(axis, by):
        return device_at(where, **{axis: shifted(where, axis, by)})

    greet([sibling] + [peer(a, k) for a in "xyz" for k in range(1, SIZE[a])])
    sender = Sender(send_sems, recv_sems)
    half = 2 * WIDTH
    left, right = slice(0, half), slice(half, 2 * half)

    core = [
        sender.send(low_ref.at[1 - c, :, :, :, part], r0.at[:, :, :, part], sibling)
        for part in (left, right)
    ]
    lane = lax.rem(lax.broadcasted_iota(jnp.int32, (16, 4 * WIDTH), 1), 16)
    diagonal = lane == lax.broadcasted_iota(jnp.int32, (16, 4 * WIDTH), 0)
    for i in range(4):
        line = prep_ref[i : i + 1, :]
        lhs[i * 16 : (i + 1) * 16, :] = jnp.where(diagonal, line, F32(0.0)).astype(BF16)

    core[0].wait_recv()
    sent_a, sent_b = [], []
    for k in (2, 1, 3, 0):
        to = shifted(where, "x", k)
        value = (low_ref[c, to, :, :, left] + r0[to, :, :, left]).reshape(32, half)
        if k:
            send_a[k - 1] = value.astype(BF16)
            sent_a.append(sender.send(send_a.at[k - 1], recv_a.at[k - 1], peer("x", k)))
        else:
            acc_a[...] = value.reshape(NY, 8, half)
    core[1].wait_recv()
    for k in (2, 1, 3, 0):
        to = shifted(where, "y", k)
        value = (low_ref[c, :, to, :, right] + r0[:, to, :, right]).reshape(32, half)
        if k:
            send_b[k - 1] = value.astype(BF16)
            sent_b.append(sender.send(send_b.at[k - 1], recv_b.at[k - 1], peer("y", k)))
        else:
            acc_b[...] = value.reshape(NX, 8, half)
    second = []
    for copies, recv, acc, recv2, axis in (
        (sent_a, recv_a, acc_a, recv2_a, "y"),
        (sent_b, recv_b, acc_b, recv2_b, "x"),
    ):
        for copy in copies:
            copy.wait_recv()
        total = (recv[0].astype(F32) + recv[1].astype(F32)) + recv[2].astype(F32)
        acc[...] = acc[...] + total.reshape(4, 8, half)
        for k in (2, 1, 3):
            to = shifted(where, axis, k)
            second.append(sender.send(acc.at[to], recv2.at[k - 1], peer(axis, k)))
    for copies, acc, recv2, axis, base in (
        (second[:3], acc_a, recv2_a, "y", 0),
        (second[3:], acc_b, recv2_b, "x", half),
    ):
        for copy in copies:
            copy.wait_recv()
        total = acc[where[axis]] + ((recv2[0] + recv2[1]) + recv2[2])
        for i in range(NZ):
            rows[i, :, base : base + half] = total[i : i + 1, :]
    third = []
    for k in (4, 3, 5, 2, 6, 1, 7):
        to = shifted(where, "z", k)
        third.append(sender.send(rows.at[to], recv3.at[k - 1], peer("z", k)))
    low = rows[z]
    for copy in third:
        copy.wait_recv()
    for k in range(NZ - 1):
        low = low + recv3[k]

    first = beta_one * first_ref[...] + (1.0 - beta_one) * low
    second_moment = beta_two * second_ref[...] + (1.0 - beta_two) * low * low
    new_first[...] = first
    new_second[...] = second_moment
    direction = (
        first
        / (1.0 - beta_one**adam_step)
        / (jnp.sqrt(second_moment / (1.0 - beta_two**adam_step)) + adam_eps)
    )
    for a in range(16):
        dir_rows[a : a + 1, :] = direction[:, a * 256 : (a + 1) * 256]
    for p in range(2):
        tiles[p, c, z, y, x] = dir_rows[:, p * 128 : (p + 1) * 128].astype(BF16)

    copies = []
    for k in (4, 3, 5, 2, 6, 1, 7):
        mine = tiles.at[:, c, z, y, x]
        copies.append(sender.send(mine, mine, peer("z", k)))
    for copy in copies:
        copy.wait_recv()
    sent = [[], []]
    for k in (2, 1, 3):
        for p, axis in ((0, "y"), (1, "x")):
            mine = tiles.at[p, c, :, y, x]
            sent[p].append(sender.send(mine, mine, peer(axis, k)))
    final, across = [], []
    for p, axis in ((0, "x"), (1, "y")):
        for copy in sent[p]:
            copy.wait_recv()
        mine = tiles.at[0, c, :, :, x] if p == 0 else tiles.at[1, c, :, y, :]
        for k in (2, 1, 3):
            final.append((p, axis, k, sender.send(mine, mine, peer(axis, k))))
        across.append(sender.send(mine, mine, sibling))
    for p, axis, k, copy in final:
        copy.wait_recv()
        at = shifted(where, axis, -k)
        got = tiles.at[0, c, :, :, at] if p == 0 else tiles.at[1, c, :, at, :]
        across.append(sender.send(got, got, sibling))
    for copy in across:
        copy.wait_recv()
    for p in range(2):
        step = dot(lhs[...], tiles[p].reshape(RANK * 16, 128))
        columns = slice(p * 128, (p + 1) * 128)
        new_master[:, columns] = master_ref[:, columns] - learn_rate * galore_scale * step
    sender.finish()


def update(low, first, second, master, prep):
    vmem = pl.BlockSpec(memory_space=pltpu.VMEM)
    half = 2 * WIDTH
    n_sems = 64
    return pl.pallas_call(
        update_kernel,
        out_shape=(
            jax.ShapeDtypeStruct((64, 256), F32),
            jax.ShapeDtypeStruct((1, 4 * WIDTH), F32),
            jax.ShapeDtypeStruct((1, 4 * WIDTH), F32),
        ),
        in_specs=[vmem] * 5,
        out_specs=(vmem, vmem, vmem),
        scratch_shapes=[
            pltpu.VMEM((NX, NY, 8, 4 * WIDTH), F32),
            pltpu.VMEM((3, 32, half), BF16),
            pltpu.VMEM((3, 32, half), BF16),
            pltpu.VMEM((3, 32, half), BF16),
            pltpu.VMEM((3, 32, half), BF16),
            pltpu.VMEM((NY, 8, half), F32),
            pltpu.VMEM((NX, 8, half), F32),
            pltpu.VMEM((3, 8, half), F32),
            pltpu.VMEM((3, 8, half), F32),
            pltpu.VMEM((NZ, 1, 4 * WIDTH), F32),
            pltpu.VMEM((NZ - 1, 1, 4 * WIDTH), F32),
            pltpu.VMEM((16, 256), F32),
            pltpu.VMEM((2, NC, NZ, NY, NX, 16, 128), BF16),
            pltpu.VMEM((64, 4 * WIDTH), BF16),
            pltpu.SemaphoreType.DMA((n_sems,)),
            pltpu.SemaphoreType.DMA((n_sems,)),
        ],
        compiler_params=pltpu.CompilerParams(
            collective_id=1, has_side_effects=True, vmem_limit_bytes=VMEM_LIMIT
        ),
        name="update",
    )(low, first, second, master, prep)


def projector_orders(projector):
    by_place = projector.reshape(4, NZ, NY, NX, NC)
    rows = by_place.transpose(0, 4, 3, 2, 1).reshape(4, RANK)
    last = by_place.transpose(0, 4, 1, 2, 3).reshape(4, RANK, 1)
    prep = jnp.broadcast_to(last, (4, RANK, 16)).reshape(4, RANK * 16)
    return rows, prep.astype(F32)


def shards(
    inputs, grad_out, norm_gain, master, projector, moment_first, moment_second, doc_lengths
):
    rows, prep = projector_orders(projector)
    weights = gather_weights(master, rows)
    weights = weights.reshape(3, NC, NZ, NY, 2, 2, 16, PART)
    low = local_terms(doc_lengths, inputs, grad_out, norm_gain[None, :], weights)
    low = low.reshape(NC, NX, NY, NZ, 4 * WIDTH)
    new_master, new_first, new_second = update(
        low, moment_first, moment_second, master.reshape(64, 256), prep
    )
    return (new_master.reshape(4, 4 * WIDTH), new_first, new_second)


def solution(mesh):
    return jax.shard_map(
        shards,
        mesh=mesh,
        in_specs=(
            P("dp", None),
            P("dp", None),
            P(),
            P("dp", None),
            P("dp", None),
            P("dp", None),
            P("dp", None),
            P("dp", None),
        ),
        out_specs=(P("dp", None), P("dp", None), P("dp", None)),
        check_vma=False,
    )
```

time: 941 us -> 152 us (0.16)
  waiting for transfers between devices: 800 us -> 0 us
  Pallas kernels: 0 us -> 143 us
  matrix products: 83.9 us -> 0 us
  between operations: 14.1 us -> 0.68 us
  other arithmetic: 12.7 us -> 0 us
  local copies, waits for them, and re-layouts: 21 us -> 8.65 us
    unnamed x6 -> x0, waiting for transfers between devices: 560 us -> none
    all_gather x2 -> x0, waiting for transfers between devices: 240 us -> none  [the longest x1 123 us: shards(): lax.all_gather(master.astype(jnp.bfloat16), 'dp', axis=0, tiled=True)]
    pallas_call x0 -> x3, Pallas kernels: none -> 143 us  [the longest x1 60.1 us: gather_weights(): pl.pallas_call(weights_kernel, out_shape=jax.ShapeDtypeStruct((3, NC, NZ,...]
    dot_general x12 -> x0, matrix products: 83.9 us -> none  [the longest x1 15.6 us: attend(): jnp.dot(grad_scores.T, queries.astype(jnp.float32), precision=highest)]
    unnamed x24 -> x8, local copies, waits for them, and re-layouts: 14.8 us -> 3.61 us
  transfers between devices with their start and end apart: 4 -> 0, of which waited for: 4 -> 0; matrix products, arithmetic and copies ran while one was open for 0% -> 0% of each run, Pallas kernels for 0% -> 0%
where the time goes in v1:
time: 152 us
  Pallas kernels  143 us (94%)
  local copies, waits for them, and re-layouts  8.65 us (6%)
    pallas_call x1, Pallas kernels, gather_weights(): pl.pallas_call(weights_kernel, out_shape=jax.ShapeDtypeStruct((3, NC, NZ,...  60.1 us
    pallas_call x1, Pallas kernels, update(): pl.pallas_call(update_kernel, out_shape=(jax.ShapeDtypeStruct((64, 256),...  46.3 us
    pallas_call x1, Pallas kernels, local_terms(): pl.pallas_call(local_kernel, out_shape=jax.ShapeDtypeStruct((RANK, 4 * WI...  36.1 us
    unnamed x8, local copies, waits for them, and re-layouts  3.61 us

profile of v1, /device:TPU:1, one launch (start us, length us, event | category | flops | bytes accessed | tf_op | source)
XLA Modules:
  0.0 151.9 jit_solution(11373482027171014034)
XLA Ops:
  0.6 0.8 copy.12
  1.5 0.3 copy.13
  1.8 0.7 reshape.31.proj_ref
  2.5 60.1 %gather_weights.1 = bf16[3,2,8,4,4,16,384]{6,5,4,3,2,1,0:T(8,128)(2,1)} custom-call(f32[4,4096]{1,0:T(4,128)} %master_ref.1, bf16[4,256]{1,0:T(4,128)(2,1)} %reshape.31.proj_ref), custom_call_target="tpu_custom_call" | custom-call | tf_op jit(solution)/shard_map/gather_weights/pallas_call | solution.py:220
  62.6 0.0 copy-start.1
  62.6 0.0 copy-start
  62.6 36.1 %local_terms.1 = f32[256,4096]{1,0:T(8,128)} custom-call(s32[1,4]{1,0:T(1,128)} %len_ref.1, bf16[384,1024]{1,0:T(8,128)(2,1)} %in_ref.1, bf16[384,1024]{1,0:T(8,128)(2,1)} %gout_ref.1, f32[1,1024]{1,0:T(1,128)} %bitcast.13, bf16[3,2,8,4,2,2,16,384]{7,6,5,4,3,2,1,0:T(8,128)(2,1)} %bitcast.9), custom_call_target="tpu_custom_call" | custom-call | tf_op jit(solution)/shard_map/local_terms/pallas_call | solution.py:360
  98.7 0.0 copy-done.1
  98.8 0.1 copy.15
  98.9 0.6 copy.14
  99.4 0.2 reshape.36
  99.6 0.2 broadcast_in_dim.9
  99.8 0.9 convert_element_type.12.prep_ref
  100.7 0.0 copy-done
  100.8 0.7 reshape.34.master_ref
  101.4 46.3 %update.1 = (f32[64,256]{1,0:T(8,128)}, f32[1,4096]{1,0:T(1,128)}, f32[1,4096]{1,0:T(1,128)}) custom-call(f32[2,4,4,8,4096]{4,3,2,1,0:T(8,128)} %bitcast.10, f32[1,4096]{1,0:T(1,128)} %first_ref.1, f32[1,4096]{1,0:T(1,128)} %second_ref.1, f32[64,256]{1,0:T(8,128)} %reshape.34.master_ref, f32[4,4096]{1,0:T(4,128)} %convert_element_type.12.prep_ref), custom_call_target="tpu_custom_call" | custom-call | tf_op jit(solution)/shard_map/update/pallas_call | solution.py:510
  147.7 1.5 reshape.35
  149.2 1.3 copy.18
  150.5 1.3 copy.19
Async XLA Ops:
  62.6 36.1 %copy-start.1 = (bf16[4,256]{1,0:T(4,128)(2,1)S(1)}, bf16[4,256]{1,0:T(4,128)(2,1)}, u32[]{:S(2)}) copy-start(bf16[4,256]{1,0:T(4,128)(2,1)} %param.12) | copy-start | bytes 6148
  62.6 38.1 %copy-start = (f32[4,4096]{1,0:T(4,128)S(1)}, f32[4,4096]{1,0:T(4,128)}, u32[]{:S(2)}) copy-start(f32[4,4096]{1,0:T(4,128)} %master_ref.1) | copy-start | bytes 196612

commit v2 on v0

v2 whole, which is shorter than its diff:
```python
import jax
import jax.numpy as jnp
import numpy as np
from jax import lax
from jax.experimental import pallas as pl
from jax.experimental.pallas import tpu as pltpu
from jax.sharding import PartitionSpec as P

NZ, NY, NX, NC = 8, 4, 4, 2
SIZE = {"z": NZ, "y": NY, "x": NX}
SHIFTS = {"z": (4, 3, 5, 2, 6, 1, 7), "y": (2, 1, 3), "x": (2, 1, 3)}
GROUPS = 4
UNIT = 256
TOK = 384
WIDTH = 1024
RANK = 256
VMEM_LIMIT = 56 * 1024 * 1024

beta_one = 0.9
beta_two = 0.999
adam_eps = 1e-08
adam_step = 10.0
learn_rate = 0.01
galore_scale = 0.25
norm_eps = 1e-05

F32 = jnp.float32
BF16 = jnp.bfloat16
MESH = pl.DeviceIdType.MESH


def place():
    me = lax.axis_index("dp")
    c = lax.rem(me, NC)
    x = lax.rem(me // NC, NX)
    y = lax.rem(me // (NC * NX), NY)
    z = me // (NC * NX * NY)
    return {"z": z, "y": y, "x": x, "c": c}


def device_at(where, **moved):
    at = dict(where, **moved)
    return ((at["z"] * NY + at["y"]) * NX + at["x"]) * NC + at["c"]


def shifted(where, axis, by):
    n = SIZE[axis]
    return lax.rem(where[axis] + (by + n), n)


class Links:
    def __init__(self, send_sems, recv_sems):
        self.send_sems, self.recv_sems = send_sems, recv_sems
        self.bases = {}
        self.used = 0

    def reserve(self, name, count):
        self.bases[name] = self.used
        self.used += count

    def copy(self, name, i, src, dst, device):
        at = self.bases[name] + i
        return pltpu.make_async_remote_copy(
            src_ref=src,
            dst_ref=dst,
            send_sem=self.send_sems.at[at],
            recv_sem=self.recv_sems.at[at],
            device_id=(device,),
            device_id_type=MESH,
        )


N_SEMS = 160


def start(copies):
    for copy in copies:
        copy.start()


def received(copies):
    for copy in copies:
        copy.wait_recv()


def sent(copies):
    for copy in copies:
        copy.wait_send()


def greet(devices):
    barrier = pltpu.get_barrier_semaphore()
    for device in devices:
        pl.semaphore_signal(barrier, inc=1, device_id=(device,), device_id_type=MESH)
    pl.semaphore_wait(barrier, len(devices))


def dot(a, b, dims=((1,), (0,))):
    return lax.dot_general(a, b, (dims, ((), ())), preferred_element_type=F32)


ROWS = ((1,), (1,))
COLS = ((0,), (0,))


def split(value):
    high = value.astype(BF16)
    return high, (value - high.astype(F32)).astype(BF16)


def adam(low, first, second):
    new_first = beta_one * first + (1.0 - beta_one) * low
    new_second = beta_two * second + (1.0 - beta_two) * low * low
    direction = (
        new_first
        / (1.0 - beta_one**adam_step)
        / (jnp.sqrt(new_second / (1.0 - beta_two**adam_step)) + adam_eps)
    )
    return new_first, new_second, direction


BLOCKS = ((0, 256, 256), (256, 384, 384))


def attend_pair(q, k, v, gh, bias_ref, masks):
    gh_high, gh_rest = split(gh)
    v_twice = jnp.concatenate([v, v], axis=1)
    out_q, out_a, out_k, out_v = [], [], [], []
    for lo, hi, keys in BLOCKS:
        parts = []
        for mask in masks:
            q_m, k_m, v_m = q[lo:hi] * mask, k[:keys] * mask, v[:keys] * mask
            s = dot(q_m, k[:keys], ROWS) * 0.125 + bias_ref[lo:hi, :keys]
            e = jnp.exp(s - jnp.max(s, axis=1, keepdims=True))
            p = e * (1.0 / jnp.sum(e, axis=1, keepdims=True))
            p_high, p_rest = split(p)
            a = dot(p_high, v_m)
            gh_m = gh_high[lo:hi] * mask
            gh_both = jnp.concatenate([gh_m, gh_rest[lo:hi] * mask], axis=1)
            gv = dot(p_high, gh_both, COLS)
            gv = gv[:, :128] + gv[:, 128:] + dot(p_rest, gh_m, COLS)
            gp = dot(gh_both, v_twice[:keys], ROWS)
            gs = p * (gp - jnp.sum(p * gp, axis=1, keepdims=True))
            gs_high, gs_rest = split(gs)
            gq = dot(gs_high, k_m) + dot(gs_rest, k_m)
            gk = dot(gs_high, q_m, COLS) + dot(gs_rest, q_m, COLS)
            parts.append((gq, a, gk, gv))
        gq, a, gk, gv = (one + two for one, two in zip(*parts))
        out_q.append(gq)
        out_a.append(a)
        out_k.append(gk)
        out_v.append(gv)

    def fold(first, second):
        return jnp.concatenate([first + second[:256], second[256:]], axis=0)

    gq = jnp.concatenate(out_q, axis=0)
    a = jnp.concatenate(out_a, axis=0)
    return gq, fold(*out_k), fold(*out_v), a


def main_kernel(
    len_ref, in_ref, gout_ref, gain_ref, master_ref, proj_ref, first_ref, second_ref,
    step_ref, low_out,
    w, quad_w, quad_p, own_p, rows_w, rows_p, order, normed, bias, np_t, gp_t,
    q_s, k_s, v_s, gh_s, low_s, r0, s1, v1, acc, v2, rows, v3, dir_rows, tiles, lhs,
    send_sems, recv_sems
):
    where = place()
    c, x, y, z = where["c"], where["x"], where["y"], where["z"]
    xh, xl = x // 2, lax.rem(x, 2)
    flip = x + 1 - 2 * xl
    sibling = device_at(where, c=1 - c)
    links = Links(send_sems, recv_sems)
    for name, count in (
        ("quad", 6), ("z", 7), ("mid0", 6), ("mid1", 6), ("bulk", 24), ("across", 32),
        ("bulk_p", 3), ("across_p", 4), ("core", 4), ("sum1", 12), ("sum2", 12),
        ("sum3", 7), ("dir_z", 7), ("dir_mid", 6), ("dir_last", 6), ("dir_across", 8),
    ):
        links.reserve(name, count)

    def peer(axis, by):
        return device_at(where, **{axis: shifted(where, axis, by)})

    greet(
        [sibling, device_at(where, x=flip, c=1 - c)]
        + [peer(axis, k) for axis in "xyz" for k in SHIFTS[axis]]
    )

    own_p[...] = proj_ref[...].astype(F32)
    mine = xl * 2 + c
    quad = []
    for i, (dx, dc) in enumerate(((0, 1), (1, 0), (1, 1))):
        to_xl = 1 - xl if dx else xl
        to_c = 1 - c if dc else c
        to = device_at(where, x=xh * 2 + to_xl, c=to_c)
        columns = pl.ds(pl.multiple_of((to_xl * 2 + to_c) * WIDTH, WIDTH), WIDTH)
        quad.append(
            links.copy("quad", 2 * i, master_ref.at[:, columns], quad_w.at[mine], to)
        )
        quad.append(links.copy("quad", 2 * i + 1, own_p, quad_p.at[mine], to))
    start(quad)
    columns = pl.ds(pl.multiple_of(mine * WIDTH, WIDTH), WIDTH)
    quad_w[mine] = master_ref[:, columns]
    quad_p[mine] = own_p[...]

    source = lax.broadcasted_iota(jnp.int32, (RANK, RANK), 0)
    place_to = lax.broadcasted_iota(jnp.int32, (RANK, RANK), 1)
    natural = (
        (place_to & 7) * 32
        + ((place_to >> 3) & 3) * 8
        + ((place_to >> 5) & 3) * 2
        + (place_to >> 7)
    )
    order[...] = (source == natural).astype(F32).astype(BF16)

    received(quad)
    for i in range(4):
        rows_w[i * 4 : i * 4 + 4, :] = quad_w[i]
        rows_p[i * 4 : i * 4 + 4, :] = quad_p[i]
    ordered = dot(rows_p[...].astype(BF16), order[...])
    w[0, 0, c, z, y, xh, xl] = jnp.where(c == 0, ordered[:, :128], ordered[:, 128:]).astype(
        BF16
    )
    w[1, 0, c, z, y, xh, xl] = jnp.zeros((16, 128), BF16)
    for pair in range(8):
        w[pair % 2, 1 + pair // 2, c, z, y, xh, xl] = rows_w[
            :, pair * 128 : (pair + 1) * 128
        ].astype(BF16)

    along_z = []
    for i, k in enumerate(SHIFTS["z"]):
        for_all = w.at[:, :, c, z, y, xh, xl]
        along_z.append(links.copy("z", i, for_all, for_all, peer("z", k)))
    start(along_z)

    values = in_ref[...].astype(F32)
    scale = lax.rsqrt(jnp.mean(values * values, axis=1, keepdims=True) + norm_eps)
    normed[...] = (values * scale * gain_ref[...]).astype(BF16)
    b0 = len_ref[0, 0]
    b1 = b0 + len_ref[0, 1]
    b2 = b1 + len_ref[0, 2]
    b3 = b2 + len_ref[0, 3]

    def segment(position):
        return sum((position >= b).astype(jnp.int32) for b in (b0, b1, b2, b3))

    row = lax.broadcasted_iota(jnp.int32, (TOK, 1), 0)
    col = lax.broadcasted_iota(jnp.int32, (1, TOK), 1)
    seen = (segment(row) == segment(col)) & (row >= col)
    bias[...] = jnp.where(seen, F32(0.0), F32(-1e30))
    received(along_z)

    def middle(name, a_slots, b_slots):
        copies = []
        for i, k in enumerate(SHIFTS["y"]):
            ref = w.at[0, a_slots, c, :, y, xh, xl]
            copies.append(links.copy(name, i, ref, ref, peer("y", k)))
        for i, k in enumerate(SHIFTS["x"]):
            ref = w.at[1, b_slots, c, :, y, xh, xl]
            copies.append(links.copy(name, 3 + i, ref, ref, peer("x", k)))
        return copies

    def along_x(slot, at):
        return w.at[0, slot, c, :, :, at // 2, lax.rem(at, 2)]

    def along_y(slot, at):
        return w.at[1, slot, c, :, at]

    def bulk(g):
        copies = []
        for i, k in enumerate(SHIFTS["x"]):
            ref = along_x(g + 1, x)
            copies.append(links.copy("bulk", g * 6 + i, ref, ref, peer("x", k)))
        for i, k in enumerate(SHIFTS["y"]):
            ref = along_y(g + 1, y)
            copies.append(links.copy("bulk", g * 6 + 3 + i, ref, ref, peer("y", k)))
        return copies

    def bulk_p():
        copies = []
        for i, k in enumerate(SHIFTS["x"]):
            ref = along_x(0, x)
            copies.append(links.copy("bulk_p", i, ref, ref, peer("x", k)))
        return copies

    def across(g):
        refs = [along_x(g + 1, x), along_y(g + 1, y)]
        refs += [along_x(g + 1, shifted(where, "x", -k)) for k in SHIFTS["x"]]
        refs += [along_y(g + 1, shifted(where, "y", -k)) for k in SHIFTS["y"]]
        return [links.copy("across", g * 8 + i, r, r, sibling) for i, r in enumerate(refs)]

    def across_p():
        refs = [along_x(0, x)] + [along_x(0, shifted(where, "x", -k)) for k in SHIFTS["x"]]
        return [links.copy("across_p", i, r, r, sibling) for i, r in enumerate(refs)]

    def open_bulk(g):
        start(bulk(g))
        start(across(g)[:2])

    def forward(g):
        for got, on in zip(bulk(g), across(g)[2:]):
            got.wait_recv()
            on.start()

    early = middle("mid0", pl.ds(0, 2), pl.ds(1, 1))
    late = middle("mid1", pl.ds(2, 3), pl.ds(2, 3))
    start(early)
    start(late)

    spread = lax.broadcasted_iota(jnp.int32, (RANK, 256), 1)
    source = lax.broadcasted_iota(jnp.int32, (RANK, 256), 0)
    diagonal = (spread & 15) == (lax.broadcasted_iota(jnp.int32, (RANK, 256), 0) & 15)
    own_rows = own_p[...].astype(BF16)
    for n in range(16):
        kk = n * 16 + (spread >> 4)
        pick = (source == ((kk & 127) * 2 + (kk >> 7))).astype(F32).astype(BF16)
        line = dot(own_rows, pick)
        for i in range(4):
            lhs[i * 16 : (i + 1) * 16, n * 256 : (n + 1) * 256] = jnp.where(
                diagonal[:16], line[i : i + 1, :], F32(0.0)
            ).astype(BF16)

    received(early)
    open_bulk(0)
    start(bulk_p())
    start(across_p()[:1])
    received(late)
    open_bulk(1)
    forward(0)
    for got, on in zip(bulk_p(), across_p()[1:]):
        got.wait_recv()
        on.start()

    lane = lax.broadcasted_iota(jnp.int32, (1, 128), 1)
    firsts = (lane < 64).astype(F32).astype(BF16)
    masks = (firsts, 1 - firsts)

    def weight(slot, low_x, core):
        halves = [w[a, slot, core, :, :, :, low_x].reshape(WIDTH, 128) for a in range(2)]
        return jnp.concatenate(halves, axis=1)

    def project(g):
        for src, low_x, core, out in (
            (normed, 0, 0, q_s), (normed, 0, 1, k_s), (normed, 1, 0, v_s), (gout_ref, 1, 1, gh_s)
        ):
            res = dot(src[...], weight(g + 1, low_x, core))
            out[0] = res[:, :128].astype(out.dtype)
            out[1] = res[:, 128:].astype(out.dtype)

    def project_rank():
        both = [w[0, 0, core, :, :, :, 0].reshape(WIDTH, 128) for core in range(2)]
        proj = jnp.concatenate(both, axis=1)
        for src, out in ((normed, np_t), (gout_ref, gp_t)):
            high, rest = split(dot(src[...], proj).T)
            out[:, :TOK] = high
            out[:, TOK:] = rest

    def core_copy(g):
        return links.copy("core", g, low_s.at[g, 1 - c], r0.at[g], sibling)

    def sum1(g):
        return [
            links.copy("sum1", g * 3 + i, s1.at[g, i], v1.at[g, i], peer("x", k))
            for i, k in enumerate(SHIFTS["x"])
        ]

    def sum2(g):
        return [
            links.copy(
                "sum2", g * 3 + i, acc.at[g, shifted(where, "y", k)], v2.at[g, i], peer("y", k)
            )
            for i, k in enumerate(SHIFTS["y"])
        ]

    def stage_one(g):
        core_copy(g).wait_recv()
        copies = sum1(g)
        for i, k in enumerate(SHIFTS["x"]):
            to = shifted(where, "x", k)
            value = low_s[g, c, to] + r0[g, to]
            s1[g, i] = value.reshape(32, 4 * UNIT).astype(BF16)
            copies[i].start()
        acc[g] = low_s[g, c, x] + r0[g, x]

    def stage_two(g):
        received(sum1(g))
        total = (v1[g, 0].astype(F32) + v1[g, 1].astype(F32)) + v1[g, 2].astype(F32)
        acc[g] = acc[g] + total.reshape(NY, 8, 4 * UNIT)
        start(sum2(g))

    def stage_three(g):
        received(sum2(g))
        total = acc[g, y] + ((v2[g, 0] + v2[g, 1]) + v2[g, 2])
        for block in range(4):
            columns = pl.ds(pl.multiple_of(block * WIDTH + g * UNIT, UNIT), UNIT)
            for i in range(NZ):
                rows[i, :, columns] = total[i : i + 1, block * UNIT : (block + 1) * UNIT]

    @pl.loop(0, 2 * GROUPS)
    def _(t):
        g, i = t // 2, lax.rem(t, 2)

        @pl.when(i == 0)
        def _():
            received(across(g))
            project(g)

            @pl.when(t == 0)
            def _():
                received(across_p())
                project_rank()

            @pl.when(t > 0)
            def _():
                stage_one(g - 1)

            @pl.when(g < GROUPS - 1)
            def _():
                forward(g + 1)

            @pl.when(g < GROUPS - 2)
            def _():
                open_bulk(g + 2)

        @pl.when((i == 1) & (g > 0))
        def _():
            stage_two(g - 1)

        gq, gk, gv, attended = attend_pair(q_s[i], k_s[i], v_s[i], gh_s[i], bias, masks)
        grads = jnp.concatenate(
            [(gq * 0.125).astype(BF16), (gk * 0.125).astype(BF16), gv.astype(BF16)], axis=1
        )
        low = dot(np_t[...], jnp.concatenate([grads, grads], axis=0))
        attended = attended.astype(BF16)
        outer = dot(gp_t[...], jnp.concatenate([attended, attended], axis=0))
        for block in range(4):
            value = outer if block == 3 else low[:, block * 128 : (block + 1) * 128]
            columns = pl.ds(pl.multiple_of(block * UNIT + i * 128, 128), 128)
            low_s[g, :, :, :, :, columns] = value.reshape(NC, NX, NY, NZ, 128)

        @pl.when(i == 1)
        def _():
            core_copy(g).start()

            @pl.when(g > 0)
            def _():
                stage_three(g - 1)

    stage_one(GROUPS - 1)
    stage_two(GROUPS - 1)
    stage_three(GROUPS - 1)
    third = []
    for i, k in enumerate(SHIFTS["z"]):
        src = rows.at[shifted(where, "z", k)]
        third.append(links.copy("sum3", i, src, v3.at[i], peer("z", k)))
    start(third)
    low = rows[z]
    received(third)
    for i in range(NZ - 1):
        low = low + v3[i]
    low_out[...] = low
    _, _, direction = adam(low, first_ref[...], second_ref[...])
    for a in range(16):
        dir_rows[a : a + 1, :] = direction[:, a * 256 : (a + 1) * 256]
    for p in range(2):
        tiles[p, c, z, y, x] = dir_rows[:, p * 128 : (p + 1) * 128].astype(BF16)

    dir_z = []
    for i, k in enumerate(SHIFTS["z"]):
        own = tiles.at[:, c, z, y, x]
        dir_z.append(links.copy("dir_z", i, own, own, peer("z", k)))
    start(dir_z)
    received(dir_z)

    def lines(p, at):
        return tiles.at[0, c, :, :, at] if p == 0 else tiles.at[1, c, :, at]

    mid, last, over = [], [], []
    for p, axis in ((0, "y"), (1, "x")):
        for i, k in enumerate(SHIFTS[axis]):
            own = tiles.at[p, c, :, y, x]
            mid.append(links.copy("dir_mid", p * 3 + i, own, own, peer(axis, k)))
    start(mid)
    for p, axis in ((0, "x"), (1, "y")):
        received(mid[3 * p : 3 * p + 3])
        own = lines(p, where[axis])
        for i, k in enumerate(SHIFTS[axis]):
            last.append(links.copy("dir_last", p * 3 + i, own, own, peer(axis, k)))
            last[-1].start()
        over.append(links.copy("dir_across", p * 4, own, own, sibling))
        over[-1].start()
    for p, axis in ((0, "x"), (1, "y")):
        for i, k in enumerate(SHIFTS[axis]):
            last[3 * p + i].wait_recv()
            got = lines(p, shifted(where, axis, -k))
            over.append(links.copy("dir_across", p * 4 + 1 + i, got, got, sibling))
            over[-1].start()
    received(over)
    for p in range(2):
        columns = slice(p * 128, (p + 1) * 128)
        step_ref[:, columns] = dot(lhs[...], tiles[p].reshape(RANK * 16, 128))

    sent(quad + along_z + early + late + bulk_p() + across_p())

    @pl.loop(0, GROUPS)
    def _(g):
        sent(bulk(g) + across(g) + [core_copy(g)] + sum1(g) + sum2(g))

    sent(third + dir_z + mid + last + over)


def main(lengths, inputs, grad_out, gain, master, projector, first, second):
    vmem = pl.BlockSpec(memory_space=pltpu.VMEM)
    return pl.pallas_call(
        main_kernel,
        out_shape=(
            jax.ShapeDtypeStruct((64, 256), F32),
            jax.ShapeDtypeStruct((1, 4 * WIDTH), F32),
        ),
        in_specs=[pl.BlockSpec(memory_space=pltpu.SMEM)] + [vmem] * 7,
        out_specs=(vmem, vmem),
        scratch_shapes=[
            pltpu.VMEM((2, 5, NC, NZ, NY, 2, 2, 16, 128), BF16),
            pltpu.VMEM((4, 4, WIDTH), F32),
            pltpu.VMEM((4, 4, RANK), F32),
            pltpu.VMEM((4, RANK), F32),
            pltpu.VMEM((16, WIDTH), F32),
            pltpu.VMEM((16, RANK), F32),
            pltpu.VMEM((RANK, RANK), BF16),
            pltpu.VMEM((TOK, WIDTH), BF16),
            pltpu.VMEM((TOK, TOK), F32),
            pltpu.VMEM((RANK, 2 * TOK), BF16),
            pltpu.VMEM((RANK, 2 * TOK), BF16),
            pltpu.VMEM((2, TOK, 128), BF16),
            pltpu.VMEM((2, TOK, 128), BF16),
            pltpu.VMEM((2, TOK, 128), BF16),
            pltpu.VMEM((2, TOK, 128), F32),
            pltpu.VMEM((GROUPS, NC, NX, NY, NZ, 4 * UNIT), F32),
            pltpu.VMEM((GROUPS, NX, NY, NZ, 4 * UNIT), F32),
            pltpu.VMEM((GROUPS, 3, 32, 4 * UNIT), BF16),
            pltpu.VMEM((GROUPS, 3, 32, 4 * UNIT), BF16),
            pltpu.VMEM((GROUPS, NY, NZ, 4 * UNIT), F32),
            pltpu.VMEM((GROUPS, 3, NZ, 4 * UNIT), F32),
            pltpu.VMEM((NZ, 1, 4 * WIDTH), F32),
            pltpu.VMEM((NZ - 1, 1, 4 * WIDTH), F32),
            pltpu.VMEM((16, 256), F32),
            pltpu.VMEM((2, NC, NZ, NY, NX, 16, 128), BF16),
            pltpu.VMEM((64, 4 * WIDTH), BF16),
            pltpu.SemaphoreType.DMA((N_SEMS,)),
            pltpu.SemaphoreType.DMA((N_SEMS,)),
        ],
        compiler_params=pltpu.CompilerParams(
            collective_id=0, has_side_effects=True, vmem_limit_bytes=VMEM_LIMIT
        ),
        name="galore_step",
    )(lengths, inputs, grad_out, gain, master, projector, first, second)


def finish_kernel(
    step_ref, low_ref, first_ref, second_ref, master_ref, new_master, new_first, new_second
):
    first, second, _ = adam(low_ref[...], first_ref[...], second_ref[...])
    new_first[...] = first
    new_second[...] = second
    for a in range(16):
        columns = slice(a * 256, (a + 1) * 256)
        for i in range(4):
            new_master[i : i + 1, columns] = (
                master_ref[i : i + 1, columns]
                - learn_rate * galore_scale * step_ref[i * 16 + a : i * 16 + a + 1, :]
            )


def finish(step, low, first, second, master):
    vmem = pl.BlockSpec(memory_space=pltpu.VMEM)
    return pl.pallas_call(
        finish_kernel,
        out_shape=(
            jax.ShapeDtypeStruct((4, 4 * WIDTH), F32),
            jax.ShapeDtypeStruct((1, 4 * WIDTH), F32),
            jax.ShapeDtypeStruct((1, 4 * WIDTH), F32),
        ),
        in_specs=[vmem] * 5,
        out_specs=(vmem, vmem, vmem),
        name="outputs",
    )(step, low, first, second, master)


def shards(
    inputs, grad_out, norm_gain, master, projector, moment_first, moment_second, doc_lengths
):
    step, low = main(
        doc_lengths, inputs, grad_out, norm_gain[None, :], master, projector,
        moment_first, moment_second,
    )
    return finish(step, low, moment_first, moment_second, master)


def solution(mesh):
    return jax.shard_map(
        shards,
        mesh=mesh,
        in_specs=(
            P("dp", None),
            P("dp", None),
            P(),
            P("dp", None),
            P("dp", None),
            P("dp", None),
            P("dp", None),
            P("dp", None),
        ),
        out_specs=(P("dp", None), P("dp", None), P("dp", None)),
        check_vma=False,
    )
```

time: 941 us -> 130 us (0.14)
  waiting for transfers between devices: 800 us -> 0 us
  Pallas kernels: 0 us -> 129 us
  matrix products: 83.9 us -> 0 us
  local copies, waits for them, and re-layouts: 21 us -> 0 us
  between operations: 14.1 us -> 0.64 us
  other arithmetic: 12.7 us -> 0 us
    unnamed x6 -> x0, waiting for transfers between devices: 560 us -> none
    all_gather x2 -> x0, waiting for transfers between devices: 240 us -> none  [the longest x1 123 us: shards(): lax.all_gather(master.astype(jnp.bfloat16), 'dp', axis=0, tiled=True)]
    pallas_call x0 -> x2, Pallas kernels: none -> 129 us  [the longest x1 128 us: main(): pl.pallas_call(main_kernel, out_shape=(jax.ShapeDtypeStruct((64, 256), F3...]
    dot_general x12 -> x0, matrix products: 83.9 us -> none  [the longest x1 15.6 us: attend(): jnp.dot(grad_scores.T, queries.astype(jnp.float32), precision=highest)]
    unnamed x24 -> x0, local copies, waits for them, and re-layouts: 14.8 us -> none
  transfers between devices with their start and end apart: 4 -> 0, of which waited for: 4 -> 0; matrix products, arithmetic and copies ran while one was open for 0% -> 0% of each run, Pallas kernels for 0% -> 0%
where the time goes in v2:
time: 130 us
  Pallas kernels  129 us (99%)
    pallas_call x1, Pallas kernels, main(): pl.pallas_call(main_kernel, out_shape=(jax.ShapeDtypeStruct((64, 256), F3...  128 us

profile of v2, /device:TPU:1, one launch (start us, length us, event | category | flops | bytes accessed | tf_op | source)
XLA Modules:
  0.0 129.8 jit_solution(18064447880630457745)
XLA Ops:
  0.6 127.6 %galore_step.1 = (f32[64,256]{1,0:T(8,128)}, f32[1,4096]{1,0:T(1,128)}) custom-call(s32[1,4]{1,0:T(1,128)} %len_ref.1, bf16[384,1024]{1,0:T(8,128)(2,1)} %in_ref.1, bf16[384,1024]{1,0:T(8,128)(2,1)} %gout_ref.1, f32[1,1024]{1,0:T(1,128)} %bitcast.1, f32[4,4096]{1,0:T(4,128)} %master_ref.3, bf16[4,256]{1,0:T(4,128)(2,1)} %proj_ref.1, f32[1,4096]{1,0:T(1,128)} %first_ref.3, ...), custom_call_target="tpu_custom_call" | custom-call | tf_op jit(solution)/shard_map/galore_step/pallas_call | solution.py:515
  128.2 1.6 %outputs.1 = (f32[4,4096]{1,0:T(4,128)}, f32[1,4096]{1,0:T(1,128)}, f32[1,4096]{1,0:T(1,128)}) custom-call(f32[64,256]{1,0:T(8,128)} %get-tuple-element.5.step_ref, f32[1,4096]{1,0:T(1,128)} %get-tuple-element.6.low_ref, f32[1,4096]{1,0:T(1,128)} %first_ref.3, f32[1,4096]{1,0:T(1,128)} %second_ref.3, f32[4,4096]{1,0:T(4,128)} %master_ref.3), custom_call_target="tpu_custom_call" | custom-call | tf_op jit(solution)/shard_map/outputs/pallas_call | solution.py:577

commit v3 on v2

--- a/solution.py
+++ b/solution.py
@@ -70,7 +70,7 @@
         )
 
 
-N_SEMS = 160
+N_SEMS = 208
 
 
 def start(copies):
@@ -173,9 +173,10 @@
     sibling = device_at(where, c=1 - c)
     links = Links(send_sems, recv_sems)
     for name, count in (
-        ("quad", 6), ("z", 7), ("mid0", 6), ("mid1", 6), ("bulk", 24), ("across", 32),
-        ("bulk_p", 3), ("across_p", 4), ("core", 4), ("sum1", 12), ("sum2", 12),
-        ("sum3", 7), ("dir_z", 7), ("dir_mid", 6), ("dir_last", 6), ("dir_across", 8),
+        ("quad", 6), ("z0", 7), ("zp", 7), ("z1", 7), ("mid0", 6), ("midp", 3), ("mid1", 6),
+        ("bulk", 24), ("across", 32), ("bulk_p", 3), ("across_p", 4), ("core", 4),
+        ("sum1", 12), ("sum2", 12), ("sum3", 14), ("dir_z", 14), ("dir_mid", 12),
+        ("dir_last", 12), ("dir_across", 16),
     ):
         links.reserve(name, count)
 
@@ -219,20 +220,25 @@
         rows_w[i * 4 : i * 4 + 4, :] = quad_w[i]
         rows_p[i * 4 : i * 4 + 4, :] = quad_p[i]
     ordered = dot(rows_p[...].astype(BF16), order[...])
-    w[0, 0, c, z, y, xh, xl] = jnp.where(c == 0, ordered[:, :128], ordered[:, 128:]).astype(
+    w[0, 4, c, z, y, xh, xl] = jnp.where(c == 0, ordered[:, :128], ordered[:, 128:]).astype(
         BF16
     )
-    w[1, 0, c, z, y, xh, xl] = jnp.zeros((16, 128), BF16)
     for pair in range(8):
-        w[pair % 2, 1 + pair // 2, c, z, y, xh, xl] = rows_w[
+        w[pair % 2, pair // 2, c, z, y, xh, xl] = rows_w[
             :, pair * 128 : (pair + 1) * 128
         ].astype(BF16)
 
-    along_z = []
-    for i, k in enumerate(SHIFTS["z"]):
-        for_all = w.at[:, :, c, z, y, xh, xl]
-        along_z.append(links.copy("z", i, for_all, for_all, peer("z", k)))
-    start(along_z)
+    def first_step(name, slots, kinds):
+        copies = []
+        for i, k in enumerate(SHIFTS["z"]):
+            ref = w.at[kinds, slots, c, z, y, xh, xl]
+            copies.append(links.copy(name, i, ref, ref, peer("z", k)))
+        return copies
+
+    z_first = first_step("z0", pl.ds(0, 1), pl.ds(0, 2))
+    z_rank = first_step("zp", pl.ds(4, 1), pl.ds(0, 1))
+    z_rest = first_step("z1", pl.ds(1, 3), pl.ds(0, 2))
+    start(z_first + z_rank + z_rest)
 
     values = in_ref[...].astype(F32)
     scale = lax.rsqrt(jnp.mean(values * values, axis=1, keepdims=True) + norm_eps)
@@ -249,16 +255,12 @@
     col = lax.broadcasted_iota(jnp.int32, (1, TOK), 1)
     seen = (segment(row) == segment(col)) & (row >= col)
     bias[...] = jnp.where(seen, F32(0.0), F32(-1e30))
-    received(along_z)
-
-    def middle(name, a_slots, b_slots):
+    def middle(name, slots, kinds):
         copies = []
-        for i, k in enumerate(SHIFTS["y"]):
-            ref = w.at[0, a_slots, c, :, y, xh, xl]
-            copies.append(links.copy(name, i, ref, ref, peer("y", k)))
-        for i, k in enumerate(SHIFTS["x"]):
-            ref = w.at[1, b_slots, c, :, y, xh, xl]
-            copies.append(links.copy(name, 3 + i, ref, ref, peer("x", k)))
+        for kind, axis in kinds:
+            for k in SHIFTS[axis]:
+                ref = w.at[kind, slots, c, :, y, xh, xl]
+                copies.append(links.copy(name, len(copies), ref, ref, peer(axis, k)))
         return copies
 
     def along_x(slot, at):
@@ -270,28 +272,28 @@
     def bulk(g):
         copies = []
         for i, k in enumerate(SHIFTS["x"]):
-            ref = along_x(g + 1, x)
+            ref = along_x(g, x)
             copies.append(links.copy("bulk", g * 6 + i, ref, ref, peer("x", k)))
         for i, k in enumerate(SHIFTS["y"]):
-            ref = along_y(g + 1, y)
+            ref = along_y(g, y)
             copies.append(links.copy("bulk", g * 6 + 3 + i, ref, ref, peer("y", k)))
         return copies
 
     def bulk_p():
         copies = []
         for i, k in enumerate(SHIFTS["x"]):
-            ref = along_x(0, x)
+            ref = along_x(4, x)
             copies.append(links.copy("bulk_p", i, ref, ref, peer("x", k)))
         return copies
 
     def across(g):
-        refs = [along_x(g + 1, x), along_y(g + 1, y)]
-        refs += [along_x(g + 1, shifted(where, "x", -k)) for k in SHIFTS["x"]]
-        refs += [along_y(g + 1, shifted(where, "y", -k)) for k in SHIFTS["y"]]
+        refs = [along_x(g, x), along_y(g, y)]
+        refs += [along_x(g, shifted(where, "x", -k)) for k in SHIFTS["x"]]
+        refs += [along_y(g, shifted(where, "y", -k)) for k in SHIFTS["y"]]
         return [links.copy("across", g * 8 + i, r, r, sibling) for i, r in enumerate(refs)]
 
     def across_p():
-        refs = [along_x(0, x)] + [along_x(0, shifted(where, "x", -k)) for k in SHIFTS["x"]]
+        refs = [along_x(4, x)] + [along_x(4, shifted(where, "x", -k)) for k in SHIFTS["x"]]
         return [links.copy("across_p", i, r, r, sibling) for i, r in enumerate(refs)]
 
     def open_bulk(g):
@@ -303,10 +305,21 @@
             got.wait_recv()
             on.start()
 
-    early = middle("mid0", pl.ds(0, 2), pl.ds(1, 1))
-    late = middle("mid1", pl.ds(2, 3), pl.ds(2, 3))
-    start(early)
-    start(late)
+    both = ((0, "y"), (1, "x"))
+    mid_first = middle("mid0", pl.ds(0, 1), both)
+    mid_rank = middle("midp", pl.ds(4, 1), both[:1])
+    mid_rest = middle("mid1", pl.ds(1, 3), both)
+    received(z_first)
+    start(mid_first)
+    received(z_rank)
+    start(mid_rank)
+    received(mid_first)
+    open_bulk(0)
+    received(mid_rank)
+    start(bulk_p())
+    start(across_p()[:1])
+    received(z_rest)
+    start(mid_rest)
 
     spread = lax.broadcasted_iota(jnp.int32, (RANK, 256), 1)
     source = lax.broadcasted_iota(jnp.int32, (RANK, 256), 0)
@@ -321,16 +334,11 @@
                 diagonal[:16], line[i : i + 1, :], F32(0.0)
             ).astype(BF16)
 
-    received(early)
-    open_bulk(0)
-    start(bulk_p())
-    start(across_p()[:1])
-    received(late)
+    forward(0)
+    received(mid_rest)
     open_bulk(1)
-    forward(0)
-    for got, on in zip(bulk_p(), across_p()[1:]):
-        got.wait_recv()
-        on.start()
+    open_bulk(2)
+    open_bulk(3)
 
     lane = lax.broadcasted_iota(jnp.int32, (1, 128), 1)
     firsts = (lane < 64).astype(F32).astype(BF16)
@@ -344,12 +352,12 @@
         for src, low_x, core, out in (
             (normed, 0, 0, q_s), (normed, 0, 1, k_s), (normed, 1, 0, v_s), (gout_ref, 1, 1, gh_s)
         ):
-            res = dot(src[...], weight(g + 1, low_x, core))
+            res = dot(src[...], weight(g, low_x, core))
             out[0] = res[:, :128].astype(out.dtype)
             out[1] = res[:, 128:].astype(out.dtype)
 
     def project_rank():
-        both = [w[0, 0, core, :, :, :, 0].reshape(WIDTH, 128) for core in range(2)]
+        both = [w[0, 4, core, :, :, :, 0].reshape(WIDTH, 128) for core in range(2)]
         proj = jnp.concatenate(both, axis=1)
         for src, out in ((normed, np_t), (gout_ref, gp_t)):
             high, rest = split(dot(src[...], proj).T)
@@ -392,10 +400,89 @@
     def stage_three(g):
         received(sum2(g))
         total = acc[g, y] + ((v2[g, 0] + v2[g, 1]) + v2[g, 2])
+        h = g // 2
         for block in range(4):
-            columns = pl.ds(pl.multiple_of(block * WIDTH + g * UNIT, UNIT), UNIT)
+            columns = pl.ds(
+                pl.multiple_of(block * 2 * UNIT + lax.rem(g, 2) * UNIT, UNIT), UNIT
+            )
             for i in range(NZ):
-                rows[i, :, columns] = total[i : i + 1, block * UNIT : (block + 1) * UNIT]
+                rows[h, i, :, columns] = total[i : i + 1, block * UNIT : (block + 1) * UNIT]
+
+    def sum3(h):
+        return [
+            links.copy(
+                "sum3", h * 7 + i, rows.at[h, shifted(where, "z", k)], v3.at[h, i], peer("z", k)
+            )
+            for i, k in enumerate(SHIFTS["z"])
+        ]
+
+    def dir_z(h):
+        own = tiles.at[h, c, z, y, x]
+        return [
+            links.copy("dir_z", h * 7 + i, own, own, peer("z", k))
+            for i, k in enumerate(SHIFTS["z"])
+        ]
+
+    def summed(h):
+        received(sum3(h))
+        low = rows[h, z]
+        for i in range(NZ - 1):
+            low = low + v3[h, i]
+        for block in range(4):
+            columns = slice(block * WIDTH + h * 512, block * WIDTH + h * 512 + 512)
+            part = low[:, block * 512 : (block + 1) * 512]
+            low_out[:, columns] = part
+            _, _, direction = adam(part, first_ref[:, columns], second_ref[:, columns])
+            for a in range(4):
+                dir_rows[block * 4 + a : block * 4 + a + 1, :] = direction[
+                    :, a * 128 : (a + 1) * 128
+                ]
+        tiles[h, c, z, y, x] = dir_rows[...].astype(BF16)
+        start(dir_z(h))
+
+    paths = ((pl.ds(0, 4), "y", "x"), (pl.ds(4, 4), "x", "y"))
+
+    def dir_mid(h):
+        copies = []
+        for depth, axis, _ in paths:
+            own = tiles.at[h, c, depth, y, x]
+            for k in SHIFTS[axis]:
+                copies.append(
+                    links.copy("dir_mid", h * 6 + len(copies), own, own, peer(axis, k))
+                )
+        return copies
+
+    def lines(h, p, at):
+        depth = paths[p][0]
+        return tiles.at[h, c, depth, :, at] if p == 0 else tiles.at[h, c, depth, at]
+
+    def dir_last(h):
+        copies = []
+        for p, (_, _, axis) in enumerate(paths):
+            own = lines(h, p, where[axis])
+            for k in SHIFTS[axis]:
+                copies.append(
+                    links.copy("dir_last", h * 6 + len(copies), own, own, peer(axis, k))
+                )
+        return copies
+
+    def dir_across(h):
+        refs = [lines(h, p, where[paths[p][2]]) for p in range(2)]
+        for p, (_, _, axis) in enumerate(paths):
+            refs += [lines(h, p, shifted(where, axis, -k)) for k in SHIFTS[axis]]
+        return [
+            links.copy("dir_across", h * 8 + i, r, r, sibling) for i, r in enumerate(refs)
+        ]
+
+    def hand_on(h):
+        for got, on in zip(dir_last(h), dir_across(h)[2:]):
+            got.wait_recv()
+            on.start()
+
+    def step_of(h):
+        received(dir_across(h))
+        columns = slice(h * 128, (h + 1) * 128)
+        step_ref[:, columns] = dot(lhs[...], tiles[h].reshape(RANK * 16, 128))
 
     @pl.loop(0, 2 * GROUPS)
     def _(t):
@@ -406,28 +493,30 @@
             received(across(g))
             project(g)
 
-            @pl.when(t == 0)
-            def _():
-                received(across_p())
-                project_rank()
-
             @pl.when(t > 0)
             def _():
                 stage_one(g - 1)
 
+        @pl.when(i == 1)
+        def _():
+            @pl.when(g > 0)
+            def _():
+                stage_two(g - 1)
+
             @pl.when(g < GROUPS - 1)
             def _():
                 forward(g + 1)
 
-            @pl.when(g < GROUPS - 2)
-            def _():
-                open_bulk(g + 2)
-
-        @pl.when((i == 1) & (g > 0))
+        gq, gk, gv, attended = attend_pair(q_s[i], k_s[i], v_s[i], gh_s[i], bias, masks)
+
+        @pl.when(t == 0)
         def _():
-            stage_two(g - 1)
-
-        gq, gk, gv, attended = attend_pair(q_s[i], k_s[i], v_s[i], gh_s[i], bias, masks)
+            for got, on in zip(bulk_p(), across_p()[1:]):
+                got.wait_recv()
+                on.start()
+            received(across_p())
+            project_rank()
+
         grads = jnp.concatenate(
             [(gq * 0.125).astype(BF16), (gk * 0.125).astype(BF16), gv.astype(BF16)], axis=1
         )
@@ -447,67 +536,43 @@
             def _():
                 stage_three(g - 1)
 
+            @pl.when(g == 2)
+            def _():
+                start(sum3(0))
+
+        @pl.when(t == 6)
+        def _():
+            summed(0)
+
+    received(dir_z(0))
+    start(dir_mid(0))
     stage_one(GROUPS - 1)
     stage_two(GROUPS - 1)
+    received(dir_mid(0))
+    start(dir_last(0))
+    start(dir_across(0)[:2])
     stage_three(GROUPS - 1)
-    third = []
-    for i, k in enumerate(SHIFTS["z"]):
-        src = rows.at[shifted(where, "z", k)]
-        third.append(links.copy("sum3", i, src, v3.at[i], peer("z", k)))
-    start(third)
-    low = rows[z]
-    received(third)
-    for i in range(NZ - 1):
-        low = low + v3[i]
-    low_out[...] = low
-    _, _, direction = adam(low, first_ref[...], second_ref[...])
-    for a in range(16):
-        dir_rows[a : a + 1, :] = direction[:, a * 256 : (a + 1) * 256]
-    for p in range(2):
-        tiles[p, c, z, y, x] = dir_rows[:, p * 128 : (p + 1) * 128].astype(BF16)
-
-    dir_z = []
-    for i, k in enumerate(SHIFTS["z"]):
-        own = tiles.at[:, c, z, y, x]
-        dir_z.append(links.copy("dir_z", i, own, own, peer("z", k)))
-    start(dir_z)
-    received(dir_z)
-
-    def lines(p, at):
-        return tiles.at[0, c, :, :, at] if p == 0 else tiles.at[1, c, :, at]
-
-    mid, last, over = [], [], []
-    for p, axis in ((0, "y"), (1, "x")):
-        for i, k in enumerate(SHIFTS[axis]):
-            own = tiles.at[p, c, :, y, x]
-            mid.append(links.copy("dir_mid", p * 3 + i, own, own, peer(axis, k)))
-    start(mid)
-    for p, axis in ((0, "x"), (1, "y")):
-        received(mid[3 * p : 3 * p + 3])
-        own = lines(p, where[axis])
-        for i, k in enumerate(SHIFTS[axis]):
-            last.append(links.copy("dir_last", p * 3 + i, own, own, peer(axis, k)))
-            last[-1].start()
-        over.append(links.copy("dir_across", p * 4, own, own, sibling))
-        over[-1].start()
-    for p, axis in ((0, "x"), (1, "y")):
-        for i, k in enumerate(SHIFTS[axis]):
-            last[3 * p + i].wait_recv()
-            got = lines(p, shifted(where, axis, -k))
-            over.append(links.copy("dir_across", p * 4 + 1 + i, got, got, sibling))
-            over[-1].start()
-    received(over)
-    for p in range(2):
-        columns = slice(p * 128, (p + 1) * 128)
-        step_ref[:, columns] = dot(lhs[...], tiles[p].reshape(RANK * 16, 128))
-
-    sent(quad + along_z + early + late + bulk_p() + across_p())
+    start(sum3(1))
+    hand_on(0)
+    summed(1)
+    step_of(0)
+    received(dir_z(1))
+    start(dir_mid(1))
+    received(dir_mid(1))
+    start(dir_last(1))
+    start(dir_across(1)[:2])
+    hand_on(1)
+    step_of(1)
+
+    sent(quad + z_first + z_rank + z_rest + mid_first + mid_rank + mid_rest)
+    sent(bulk_p() + across_p())
 
     @pl.loop(0, GROUPS)
     def _(g):
         sent(bulk(g) + across(g) + [core_copy(g)] + sum1(g) + sum2(g))
 
-    sent(third + dir_z + mid + last + over)
+    for h in range(2):
+        sent(sum3(h) + dir_z(h) + dir_mid(h) + dir_last(h) + dir_across(h))
 
 
 def main(lengths, inputs, grad_out, gain, master, projector, first, second):
@@ -542,9 +607,9 @@
             pltpu.VMEM((GROUPS, 3, 32, 4 * UNIT), BF16),
             pltpu.VMEM((GROUPS, NY, NZ, 4 * UNIT), F32),
             pltpu.VMEM((GROUPS, 3, NZ, 4 * UNIT), F32),
-            pltpu.VMEM((NZ, 1, 4 * WIDTH), F32),
-            pltpu.VMEM((NZ - 1, 1, 4 * WIDTH), F32),
-            pltpu.VMEM((16, 256), F32),
+            pltpu.VMEM((2, NZ, 1, 2 * WIDTH), F32),
+            pltpu.VMEM((2, NZ - 1, 1, 2 * WIDTH), F32),
+            pltpu.VMEM((16, 128), F32),
             pltpu.VMEM((2, NC, NZ, NY, NX, 16, 128), BF16),
             pltpu.VMEM((64, 4 * WIDTH), BF16),
             pltpu.SemaphoreType.DMA((N_SEMS,)),
@@ -564,12 +629,15 @@
     new_first[...] = first
     new_second[...] = second
     for a in range(16):
-        columns = slice(a * 256, (a + 1) * 256)
-        for i in range(4):
-            new_master[i : i + 1, columns] = (
-                master_ref[i : i + 1, columns]
-                - learn_rate * galore_scale * step_ref[i * 16 + a : i * 16 + a + 1, :]
-            )
+        for h in range(2):
+            at = (a // 4) * WIDTH + h * 512 + (a % 4) * 128
+            columns = slice(at, at + 128)
+            for i in range(4):
+                row = i * 16 + a
+                new_master[i : i + 1, columns] = (
+                    master_ref[i : i + 1, columns]
+                    - learn_rate * galore_scale * step_ref[row : row + 1, h * 128 : h * 128 + 128]
+                )
 
 
 def finish(step, low, first, second, master):

time: 130 us -> 127 us (0.977)
  Pallas kernels: 129 us -> 126 us
    pallas_call x1, Pallas kernels: 128 us -> 125 us  [main(): pl.pallas_call(main_kernel, out_shape=(jax.ShapeDtypeStruct((64, 256), F3...]
where the time goes in v3:
time: 127 us
  Pallas kernels  126 us (99%)
    pallas_call x1, Pallas kernels, main(): pl.pallas_call(main_kernel, out_shape=(jax.ShapeDtypeStruct((64, 256), F3...  125 us

profile of v3, /device:TPU:1, one launch (start us, length us, event | category | flops | bytes accessed | tf_op | source)
XLA Modules:
  0.0 126.8 jit_solution(9434707762073940392)
XLA Ops:
  0.6 124.5 %galore_step.1 = (f32[64,256]{1,0:T(8,128)}, f32[1,4096]{1,0:T(1,128)}) custom-call(s32[1,4]{1,0:T(1,128)} %len_ref.1, bf16[384,1024]{1,0:T(8,128)(2,1)} %in_ref.1, bf16[384,1024]{1,0:T(8,128)(2,1)} %gout_ref.1, f32[1,1024]{1,0:T(1,128)} %bitcast.1, f32[4,4096]{1,0:T(4,128)} %master_ref.3, bf16[4,256]{1,0:T(4,128)(2,1)} %proj_ref.1, f32[1,4096]{1,0:T(1,128)} %first_ref.3, ...), custom_call_target="tpu_custom_call" | custom-call | tf_op jit(solution)/shard_map/galore_step/pallas_call | solution.py:580
  125.2 1.7 %outputs.1 = (f32[4,4096]{1,0:T(4,128)}, f32[1,4096]{1,0:T(1,128)}, f32[1,4096]{1,0:T(1,128)}) custom-call(f32[64,256]{1,0:T(8,128)} %get-tuple-element.5.step_ref, f32[1,4096]{1,0:T(1,128)} %get-tuple-element.6.low_ref, f32[1,4096]{1,0:T(1,128)} %first_ref.3, f32[1,4096]{1,0:T(1,128)} %second_ref.3, f32[4,4096]{1,0:T(4,128)} %master_ref.3), custom_call_target="tpu_custom_call" | custom-call | tf_op jit(solution)/shard_map/outputs/pallas_call | solution.py:645

commit v4 on v3

--- a/solution.py
+++ b/solution.py
@@ -70,7 +70,7 @@
         )
 
 
-N_SEMS = 208
+N_SEMS = 232
 
 
 def start(copies):
@@ -119,44 +119,35 @@
     return new_first, new_second, direction
 
 
-BLOCKS = ((0, 256, 256), (256, 384, 384))
-
-
-def attend_pair(q, k, v, gh, bias_ref, masks):
+def attend_pair(q, k, v, gh, bias_ref, masks, between):
+    probs, highs = [], []
+    left_v, right_v = [], []
+    for mask in masks:
+        s = dot(k, q * mask, ROWS) * 0.125 + bias_ref[...]
+        e = jnp.exp(s - jnp.max(s, axis=0, keepdims=True))
+        p = e * (1.0 / jnp.sum(e, axis=0, keepdims=True))
+        probs.append(p)
+    between()
     gh_high, gh_rest = split(gh)
     v_twice = jnp.concatenate([v, v], axis=1)
-    out_q, out_a, out_k, out_v = [], [], [], []
-    for lo, hi, keys in BLOCKS:
-        parts = []
-        for mask in masks:
-            q_m, k_m, v_m = q[lo:hi] * mask, k[:keys] * mask, v[:keys] * mask
-            s = dot(q_m, k[:keys], ROWS) * 0.125 + bias_ref[lo:hi, :keys]
-            e = jnp.exp(s - jnp.max(s, axis=1, keepdims=True))
-            p = e * (1.0 / jnp.sum(e, axis=1, keepdims=True))
-            p_high, p_rest = split(p)
-            a = dot(p_high, v_m)
-            gh_m = gh_high[lo:hi] * mask
-            gh_both = jnp.concatenate([gh_m, gh_rest[lo:hi] * mask], axis=1)
-            gv = dot(p_high, gh_both, COLS)
-            gv = gv[:, :128] + gv[:, 128:] + dot(p_rest, gh_m, COLS)
-            gp = dot(gh_both, v_twice[:keys], ROWS)
-            gs = p * (gp - jnp.sum(p * gp, axis=1, keepdims=True))
-            gs_high, gs_rest = split(gs)
-            gq = dot(gs_high, k_m) + dot(gs_rest, k_m)
-            gk = dot(gs_high, q_m, COLS) + dot(gs_rest, q_m, COLS)
-            parts.append((gq, a, gk, gv))
-        gq, a, gk, gv = (one + two for one, two in zip(*parts))
-        out_q.append(gq)
-        out_a.append(a)
-        out_k.append(gk)
-        out_v.append(gv)
-
-    def fold(first, second):
-        return jnp.concatenate([first + second[:256], second[256:]], axis=0)
-
-    gq = jnp.concatenate(out_q, axis=0)
-    a = jnp.concatenate(out_a, axis=0)
-    return gq, fold(*out_k), fold(*out_v), a
+    grads, right_k, left_q = [], [], []
+    for p, mask in zip(probs, masks):
+        p_high, p_rest = split(p)
+        gh_m, gh_r = gh_high * mask, gh_rest * mask
+        gp = dot(v_twice, jnp.concatenate([gh_m, gh_r], axis=1), ROWS)
+        gs = p * (gp - jnp.sum(p * gp, axis=0, keepdims=True))
+        highs.append(p_high)
+        left_v += [p_high, p_rest, p_high]
+        right_v += [gh_m, gh_m, gh_r]
+        grads += list(split(gs))
+        right_k += [q * mask] * 2
+        left_q += [k * mask] * 2
+    gv = dot(jnp.concatenate(left_v, axis=1), jnp.concatenate(right_v, axis=0))
+    gk = dot(jnp.concatenate(grads, axis=1), jnp.concatenate(right_k, axis=0))
+    gq_t = dot(jnp.concatenate(left_q, axis=0), jnp.concatenate(grads, axis=0), COLS)
+    by_head = jnp.concatenate([v * mask for mask in masks], axis=0)
+    a_t = dot(by_head, jnp.concatenate(highs, axis=0), COLS)
+    return gq_t, gk, gv, a_t
 
 
 def main_kernel(
@@ -173,8 +164,9 @@
     sibling = device_at(where, c=1 - c)
     links = Links(send_sems, recv_sems)
     for name, count in (
-        ("quad", 6), ("z0", 7), ("zp", 7), ("z1", 7), ("mid0", 6), ("midp", 3), ("mid1", 6),
-        ("bulk", 24), ("across", 32), ("bulk_p", 3), ("across_p", 4), ("core", 4),
+        ("quad", 6), ("z0", 7), ("zp", 7), ("z1", 7), ("mid0", 6), ("midp", 6), ("mid1", 6), ("mid2", 6),
+        ("mid3", 6),
+        ("bulk", 24), ("across", 32), ("bulk_p", 6), ("across_p", 8), ("core", 4),
         ("sum1", 12), ("sum2", 12), ("sum3", 14), ("dir_z", 14), ("dir_mid", 12),
         ("dir_last", 12), ("dir_across", 16),
     ):
@@ -251,17 +243,32 @@
     def segment(position):
         return sum((position >= b).astype(jnp.int32) for b in (b0, b1, b2, b3))
 
-    row = lax.broadcasted_iota(jnp.int32, (TOK, 1), 0)
-    col = lax.broadcasted_iota(jnp.int32, (1, TOK), 1)
-    seen = (segment(row) == segment(col)) & (row >= col)
+    key = lax.broadcasted_iota(jnp.int32, (TOK, 1), 0)
+    query = lax.broadcasted_iota(jnp.int32, (1, TOK), 1)
+    seen = (segment(key) == segment(query)) & (query >= key)
     bias[...] = jnp.where(seen, F32(0.0), F32(-1e30))
-    def middle(name, slots, kinds):
+    def middle(g):
         copies = []
-        for kind, axis in kinds:
+        for kind, axis in ((0, "y"), (1, "x")):
             for k in SHIFTS[axis]:
-                ref = w.at[kind, slots, c, :, y, xh, xl]
-                copies.append(links.copy(name, len(copies), ref, ref, peer(axis, k)))
+                ref = w.at[kind, g, c, :, y, xh, xl]
+                copies.append(links.copy("mid%d" % g, len(copies), ref, ref, peer(axis, k)))
         return copies
+
+    depths = (pl.ds(0, 4), pl.ds(4, 4))
+
+    def middle_p():
+        copies = []
+        for depth, axis in zip(depths, "yx"):
+            for k in SHIFTS[axis]:
+                ref = w.at[0, 4, c, depth, y, xh, xl]
+                copies.append(links.copy("midp", len(copies), ref, ref, peer(axis, k)))
+        return copies
+
+    def rank_lines(p, at):
+        if p == 0:
+            return w.at[0, 4, c, depths[0], :, at // 2, lax.rem(at, 2)]
+        return w.at[0, 4, c, depths[1], at]
 
     def along_x(slot, at):
         return w.at[0, slot, c, :, :, at // 2, lax.rem(at, 2)]
@@ -281,9 +288,10 @@
 
     def bulk_p():
         copies = []
-        for i, k in enumerate(SHIFTS["x"]):
-            ref = along_x(4, x)
-            copies.append(links.copy("bulk_p", i, ref, ref, peer("x", k)))
+        for p, axis in enumerate("xy"):
+            ref = rank_lines(p, where[axis])
+            for k in SHIFTS[axis]:
+                copies.append(links.copy("bulk_p", len(copies), ref, ref, peer(axis, k)))
         return copies
 
     def across(g):
@@ -293,7 +301,9 @@
         return [links.copy("across", g * 8 + i, r, r, sibling) for i, r in enumerate(refs)]
 
     def across_p():
-        refs = [along_x(4, x)] + [along_x(4, shifted(where, "x", -k)) for k in SHIFTS["x"]]
+        refs = [rank_lines(0, x), rank_lines(1, y)]
+        for p, axis in enumerate("xy"):
+            refs += [rank_lines(p, shifted(where, axis, -k)) for k in SHIFTS[axis]]
         return [links.copy("across_p", i, r, r, sibling) for i, r in enumerate(refs)]
 
     def open_bulk(g):
@@ -305,21 +315,19 @@
             got.wait_recv()
             on.start()
 
-    both = ((0, "y"), (1, "x"))
-    mid_first = middle("mid0", pl.ds(0, 1), both)
-    mid_rank = middle("midp", pl.ds(4, 1), both[:1])
-    mid_rest = middle("mid1", pl.ds(1, 3), both)
+    mids = [middle(g) for g in range(GROUPS)]
+    mid_rank = middle_p()
     received(z_first)
-    start(mid_first)
+    start(mids[0])
     received(z_rank)
     start(mid_rank)
-    received(mid_first)
+    received(mids[0])
     open_bulk(0)
+    received(z_rest)
+    start(mids[1])
     received(mid_rank)
     start(bulk_p())
-    start(across_p()[:1])
-    received(z_rest)
-    start(mid_rest)
+    start(across_p()[:2])
 
     spread = lax.broadcasted_iota(jnp.int32, (RANK, 256), 1)
     source = lax.broadcasted_iota(jnp.int32, (RANK, 256), 0)
@@ -335,10 +343,10 @@
             ).astype(BF16)
 
     forward(0)
-    received(mid_rest)
+    received(mids[1])
     open_bulk(1)
-    open_bulk(2)
-    open_bulk(3)
+    start(mids[2])
+    start(mids[3])
 
     lane = lax.broadcasted_iota(jnp.int32, (1, 128), 1)
     firsts = (lane < 64).astype(F32).astype(BF16)
@@ -503,30 +511,43 @@
             def _():
                 stage_two(g - 1)
 
-            @pl.when(g < GROUPS - 1)
+            for later in (2, 3):
+
+                @pl.when(g == later - 2)
+                def _():
+                    received(mids[later])
+                    open_bulk(later)
+
+        def between():
+            @pl.when((i == 1) & (g < GROUPS - 1))
             def _():
                 forward(g + 1)
 
-        gq, gk, gv, attended = attend_pair(q_s[i], k_s[i], v_s[i], gh_s[i], bias, masks)
+            @pl.when(t == 0)
+            def _():
+                for got, on in zip(bulk_p(), across_p()[2:]):
+                    got.wait_recv()
+                    on.start()
+
+        gq_t, gk, gv, attended_t = attend_pair(
+            q_s[i], k_s[i], v_s[i], gh_s[i], bias, masks, between
+        )
 
         @pl.when(t == 0)
         def _():
-            for got, on in zip(bulk_p(), across_p()[1:]):
-                got.wait_recv()
-                on.start()
             received(across_p())
             project_rank()
 
-        grads = jnp.concatenate(
-            [(gq * 0.125).astype(BF16), (gk * 0.125).astype(BF16), gv.astype(BF16)], axis=1
-        )
-        low = dot(np_t[...], jnp.concatenate([grads, grads], axis=0))
-        attended = attended.astype(BF16)
-        outer = dot(gp_t[...], jnp.concatenate([attended, attended], axis=0))
+        gq_t = (gq_t * 0.125).astype(BF16)
+        low_q = dot(np_t[...], jnp.concatenate([gq_t, gq_t], axis=1), ROWS)
+        grads = jnp.concatenate([(gk * 0.125).astype(BF16), gv.astype(BF16)], axis=1)
+        low_kv = dot(np_t[...], jnp.concatenate([grads, grads], axis=0))
+        attended_t = attended_t.astype(BF16)
+        outer = dot(gp_t[...], jnp.concatenate([attended_t, attended_t], axis=1), ROWS)
+        values = (low_q, low_kv[:, :128], low_kv[:, 128:], outer)
         for block in range(4):
-            value = outer if block == 3 else low[:, block * 128 : (block + 1) * 128]
             columns = pl.ds(pl.multiple_of(block * UNIT + i * 128, 128), 128)
-            low_s[g, :, :, :, :, columns] = value.reshape(NC, NX, NY, NZ, 128)
+            low_s[g, :, :, :, :, columns] = values[block].reshape(NC, NX, NY, NZ, 128)
 
         @pl.when(i == 1)
         def _():
@@ -564,7 +585,9 @@
     hand_on(1)
     step_of(1)
 
-    sent(quad + z_first + z_rank + z_rest + mid_first + mid_rank + mid_rest)
+    sent(quad + z_first + z_rank + z_rest + mid_rank)
+    for copies in mids:
+        sent(copies)
     sent(bulk_p() + across_p())
 
     @pl.loop(0, GROUPS)

time: 127 us -> 115 us (0.906)
  Pallas kernels: 126 us -> 115 us
    pallas_call x1, Pallas kernels: 125 us -> 113 us  [main(): pl.pallas_call(main_kernel, out_shape=(jax.ShapeDtypeStruct((64, 256), F3...]
where the time goes in v4:
time: 115 us
  Pallas kernels  115 us (100%)
    pallas_call x1, Pallas kernels, main(): pl.pallas_call(main_kernel, out_shape=(jax.ShapeDtypeStruct((64, 256), F3...  113 us

profile of v4, /device:TPU:1, one launch (start us, length us, event | category | flops | bytes accessed | tf_op | source)
XLA Modules:
  0.0 115.2 jit_solution(11186065295894151189)
XLA Ops:
  0.6 112.9 %galore_step.1 = (f32[64,256]{1,0:T(8,128)}, f32[1,4096]{1,0:T(1,128)}) custom-call(s32[1,4]{1,0:T(1,128)} %len_ref.1, bf16[384,1024]{1,0:T(8,128)(2,1)} %in_ref.1, bf16[384,1024]{1,0:T(8,128)(2,1)} %gout_ref.1, f32[1,1024]{1,0:T(1,128)} %bitcast.1, f32[4,4096]{1,0:T(4,128)} %master_ref.3, bf16[4,256]{1,0:T(4,128)(2,1)} %proj_ref.1, f32[1,4096]{1,0:T(1,128)} %first_ref.3, ...), custom_call_target="tpu_custom_call" | custom-call | tf_op jit(solution)/shard_map/galore_step/pallas_call | solution.py:603
  113.5 1.7 %outputs.1 = (f32[4,4096]{1,0:T(4,128)}, f32[1,4096]{1,0:T(1,128)}, f32[1,4096]{1,0:T(1,128)}) custom-call(f32[64,256]{1,0:T(8,128)} %get-tuple-element.5.step_ref, f32[1,4096]{1,0:T(1,128)} %get-tuple-element.6.low_ref, f32[1,4096]{1,0:T(1,128)} %first_ref.3, f32[1,4096]{1,0:T(1,128)} %second_ref.3, f32[4,4096]{1,0:T(4,128)} %master_ref.3), custom_call_target="tpu_custom_call" | custom-call | tf_op jit(solution)/shard_map/outputs/pallas_call | solution.py:668

commit v5 on v4

--- a/solution.py
+++ b/solution.py
@@ -165,7 +165,8 @@
     links = Links(send_sems, recv_sems)
     for name, count in (
         ("quad", 6), ("z0", 7), ("zp", 7), ("z1", 7), ("mid0", 6), ("midp", 6), ("mid1", 6), ("mid2", 6),
-        ("mid3", 6),
+        ("x3", 3),
+        ("y3", 3), ("z3", 7),
         ("bulk", 24), ("across", 32), ("bulk_p", 6), ("across_p", 8), ("core", 4),
         ("sum1", 12), ("sum2", 12), ("sum3", 14), ("dir_z", 14), ("dir_mid", 12),
         ("dir_last", 12), ("dir_across", 16),
@@ -229,8 +230,17 @@
 
     z_first = first_step("z0", pl.ds(0, 1), pl.ds(0, 2))
     z_rank = first_step("zp", pl.ds(4, 1), pl.ds(0, 1))
-    z_rest = first_step("z1", pl.ds(1, 3), pl.ds(0, 2))
-    start(z_first + z_rank + z_rest)
+    z_rest = first_step("z1", pl.ds(1, 2), pl.ds(0, 2))
+
+    def other_way(name, axis, ref):
+        return [
+            links.copy(name, i, ref, ref, peer(axis, k)) for i, k in enumerate(SHIFTS[axis])
+        ]
+
+    x_last = other_way("x3", "x", w.at[:, 3, c, z, y, xh, xl])
+    y_last = other_way("y3", "y", w.at[:, 3, c, z, y])
+    z_last = other_way("z3", "z", w.at[:, 3, c, z])
+    start(z_first + z_rank + x_last + z_rest)
 
     values = in_ref[...].astype(F32)
     scale = lax.rsqrt(jnp.mean(values * values, axis=1, keepdims=True) + norm_eps)
@@ -315,12 +325,19 @@
             got.wait_recv()
             on.start()
 
-    mids = [middle(g) for g in range(GROUPS)]
+    def across_last():
+        refs = [w.at[:, 3, c, z]]
+        refs += [w.at[:, 3, c, shifted(where, "z", -k)] for k in SHIFTS["z"]]
+        return [links.copy("across", 24 + i, r, r, sibling) for i, r in enumerate(refs)]
+
+    mids = [middle(g) for g in range(GROUPS - 1)]
     mid_rank = middle_p()
     received(z_first)
     start(mids[0])
     received(z_rank)
     start(mid_rank)
+    received(x_last)
+    start(y_last)
     received(mids[0])
     open_bulk(0)
     received(z_rest)
@@ -328,6 +345,9 @@
     received(mid_rank)
     start(bulk_p())
     start(across_p()[:2])
+    received(y_last)
+    start(z_last)
+    start(across_last()[:1])
 
     spread = lax.broadcasted_iota(jnp.int32, (RANK, 256), 1)
     source = lax.broadcasted_iota(jnp.int32, (RANK, 256), 0)
@@ -346,7 +366,6 @@
     received(mids[1])
     open_bulk(1)
     start(mids[2])
-    start(mids[3])
 
     lane = lax.broadcasted_iota(jnp.int32, (1, 128), 1)
     firsts = (lane < 64).astype(F32).astype(BF16)
@@ -498,7 +517,14 @@
 
         @pl.when(i == 0)
         def _():
-            received(across(g))
+            @pl.when(g < GROUPS - 1)
+            def _():
+                received(across(g))
+
+            @pl.when(g == GROUPS - 1)
+            def _():
+                received(across_last())
+
             project(g)
 
             @pl.when(t > 0)
@@ -511,17 +537,21 @@
             def _():
                 stage_two(g - 1)
 
-            for later in (2, 3):
-
-                @pl.when(g == later - 2)
-                def _():
-                    received(mids[later])
-                    open_bulk(later)
+            @pl.when(g == 0)
+            def _():
+                received(mids[2])
+                open_bulk(2)
 
         def between():
-            @pl.when((i == 1) & (g < GROUPS - 1))
+            @pl.when((i == 1) & (g < GROUPS - 2))
             def _():
                 forward(g + 1)
+
+            @pl.when((i == 1) & (g == GROUPS - 2))
+            def _():
+                for got, on in zip(z_last, across_last()[1:]):
+                    got.wait_recv()
+                    on.start()
 
             @pl.when(t == 0)
             def _():
@@ -565,9 +595,9 @@
         def _():
             summed(0)
 
+    stage_one(GROUPS - 1)
     received(dir_z(0))
     start(dir_mid(0))
-    stage_one(GROUPS - 1)
     stage_two(GROUPS - 1)
     received(dir_mid(0))
     start(dir_last(0))
@@ -592,7 +622,13 @@
 
     @pl.loop(0, GROUPS)
     def _(g):
-        sent(bulk(g) + across(g) + [core_copy(g)] + sum1(g) + sum2(g))
+        sent([core_copy(g)] + sum1(g) + sum2(g))
+
+        @pl.when(g < GROUPS - 1)
+        def _():
+            sent(bulk(g) + across(g))
+
+    sent(x_last + y_last + z_last + across_last())
 
     for h in range(2):
         sent(sum3(h) + dir_z(h) + dir_mid(h) + dir_last(h) + dir_across(h))

time: 115 us -> 114 us (level)
  Pallas kernels: 115 us -> 113 us
    pallas_call x1, Pallas kernels: 113 us -> 111 us  [main(): pl.pallas_call(main_kernel, out_shape=(jax.ShapeDtypeStruct((64, 256), F3...]
where the time goes in v5:
time: 114 us; the launch traced here: 113 us
  Pallas kernels  113 us (99%)
    pallas_call x1, Pallas kernels, main(): pl.pallas_call(main_kernel, out_shape=(jax.ShapeDtypeStruct((64, 256), F3...  111 us

profile of v5, /device:TPU:1, one launch (start us, length us, event | category | flops | bytes accessed | tf_op | source)
XLA Modules:
  0.0 113.4 jit_solution(1994257698694883713)
XLA Ops:
  0.6 111.1 %galore_step.1 = (f32[64,256]{1,0:T(8,128)}, f32[1,4096]{1,0:T(1,128)}) custom-call(s32[1,4]{1,0:T(1,128)} %len_ref.1, bf16[384,1024]{1,0:T(8,128)(2,1)} %in_ref.1, bf16[384,1024]{1,0:T(8,128)(2,1)} %gout_ref.1, f32[1,1024]{1,0:T(1,128)} %bitcast.1, f32[4,4096]{1,0:T(4,128)} %master_ref.3, bf16[4,256]{1,0:T(4,128)(2,1)} %proj_ref.1, f32[1,4096]{1,0:T(1,128)} %first_ref.3, ...), custom_call_target="tpu_custom_call" | custom-call | tf_op jit(solution)/shard_map/galore_step/pallas_call | solution.py:639
  111.8 1.7 %outputs.1 = (f32[4,4096]{1,0:T(4,128)}, f32[1,4096]{1,0:T(1,128)}, f32[1,4096]{1,0:T(1,128)}) custom-call(f32[64,256]{1,0:T(8,128)} %get-tuple-element.5.step_ref, f32[1,4096]{1,0:T(1,128)} %get-tuple-element.6.low_ref, f32[1,4096]{1,0:T(1,128)} %first_ref.3, f32[1,4096]{1,0:T(1,128)} %second_ref.3, f32[4,4096]{1,0:T(4,128)} %master_ref.3), custom_call_target="tpu_custom_call" | custom-call | tf_op jit(solution)/shard_map/outputs/pallas_call | solution.py:704

commit v6 on v5

--- a/solution.py
+++ b/solution.py
@@ -358,7 +358,8 @@
         pick = (source == ((kk & 127) * 2 + (kk >> 7))).astype(F32).astype(BF16)
         line = dot(own_rows, pick)
         for i in range(4):
-            lhs[i * 16 : (i + 1) * 16, n * 256 : (n + 1) * 256] = jnp.where(
+            columns = slice(n % 8 * 256, n % 8 * 256 + 256)
+            lhs[n // 8, i * 16 : (i + 1) * 16, columns] = jnp.where(
                 diagonal[:16], line[i : i + 1, :], F32(0.0)
             ).astype(BF16)
 
@@ -507,9 +508,10 @@
             on.start()
 
     def step_of(h):
+        columns = slice(h * 128, (h + 1) * 128)
+        own = dot(lhs[c], tiles[h, c].reshape(RANK * 8, 128))
         received(dir_across(h))
-        columns = slice(h * 128, (h + 1) * 128)
-        step_ref[:, columns] = dot(lhs[...], tiles[h].reshape(RANK * 16, 128))
+        step_ref[:, columns] = own + dot(lhs[1 - c], tiles[h, 1 - c].reshape(RANK * 8, 128))
 
     @pl.loop(0, 2 * GROUPS)
     def _(t):
@@ -527,22 +529,18 @@
 
             project(g)
 
-            @pl.when(t > 0)
-            def _():
-                stage_one(g - 1)
-
         @pl.when(i == 1)
         def _():
-            @pl.when(g > 0)
-            def _():
-                stage_two(g - 1)
-
             @pl.when(g == 0)
             def _():
                 received(mids[2])
                 open_bulk(2)
 
         def between():
+            @pl.when((i == 0) & (g > 0))
+            def _():
+                stage_one(g - 1)
+
             @pl.when((i == 1) & (g < GROUPS - 2))
             def _():
                 forward(g + 1)
@@ -585,30 +583,32 @@
 
             @pl.when(g > 0)
             def _():
-                stage_three(g - 1)
-
-            @pl.when(g == 2)
+                stage_two(g - 1)
+
+        @pl.when((i == 0) & (g > 1))
+        def _():
+            stage_three(g - 2)
+
+            @pl.when(g == 3)
             def _():
                 start(sum3(0))
 
-        @pl.when(t == 6)
-        def _():
-            summed(0)
-
     stage_one(GROUPS - 1)
+    stage_three(GROUPS - 2)
+    summed(0)
+    stage_two(GROUPS - 1)
+    stage_three(GROUPS - 1)
+    start(sum3(1))
     received(dir_z(0))
     start(dir_mid(0))
-    stage_two(GROUPS - 1)
     received(dir_mid(0))
     start(dir_last(0))
     start(dir_across(0)[:2])
-    stage_three(GROUPS - 1)
-    start(sum3(1))
+    summed(1)
     hand_on(0)
-    summed(1)
-    step_of(0)
     received(dir_z(1))
     start(dir_mid(1))
+    step_of(0)
     received(dir_mid(1))
     start(dir_last(1))
     start(dir_across(1)[:2])
@@ -670,7 +670,7 @@
             pltpu.VMEM((2, NZ - 1, 1, 2 * WIDTH), F32),
             pltpu.VMEM((16, 128), F32),
             pltpu.VMEM((2, NC, NZ, NY, NX, 16, 128), BF16),
-            pltpu.VMEM((64, 4 * WIDTH), BF16),
+            pltpu.VMEM((NC, 64, 2 * WIDTH), BF16),
             pltpu.SemaphoreType.DMA((N_SEMS,)),
             pltpu.SemaphoreType.DMA((N_SEMS,)),
         ],

time: 114 us -> 103 us (0.904)
  Pallas kernels: 113 us -> 103 us
    pallas_call x1, Pallas kernels: 111 us -> 101 us  [main(): pl.pallas_call(main_kernel, out_shape=(jax.ShapeDtypeStruct((64, 256), F3...]
where the time goes in v6:
time: 103 us
  Pallas kernels  103 us (100%)
    pallas_call x1, Pallas kernels, main(): pl.pallas_call(main_kernel, out_shape=(jax.ShapeDtypeStruct((64, 256), F3...  101 us

profile of v6, /device:TPU:1, one launch (start us, length us, event | category | flops | bytes accessed | tf_op | source)
XLA Modules:
  0.0 103.2 jit_solution(17679310350215090801)
XLA Ops:
  0.6 100.9 %galore_step.1 = (f32[64,256]{1,0:T(8,128)}, f32[1,4096]{1,0:T(1,128)}) custom-call(s32[1,4]{1,0:T(1,128)} %len_ref.1, bf16[384,1024]{1,0:T(8,128)(2,1)} %in_ref.1, bf16[384,1024]{1,0:T(8,128)(2,1)} %gout_ref.1, f32[1,1024]{1,0:T(1,128)} %bitcast.1, f32[4,4096]{1,0:T(4,128)} %master_ref.3, bf16[4,256]{1,0:T(4,128)(2,1)} %proj_ref.1, f32[1,4096]{1,0:T(1,128)} %first_ref.3, ...), custom_call_target="tpu_custom_call" | custom-call | tf_op jit(solution)/shard_map/galore_step/pallas_call | solution.py:639
  101.6 1.7 %outputs.1 = (f32[4,4096]{1,0:T(4,128)}, f32[1,4096]{1,0:T(1,128)}, f32[1,4096]{1,0:T(1,128)}) custom-call(f32[64,256]{1,0:T(8,128)} %get-tuple-element.5.step_ref, f32[1,4096]{1,0:T(1,128)} %get-tuple-element.6.low_ref, f32[1,4096]{1,0:T(1,128)} %first_ref.3, f32[1,4096]{1,0:T(1,128)} %second_ref.3, f32[4,4096]{1,0:T(4,128)} %master_ref.3), custom_call_target="tpu_custom_call" | custom-call | tf_op jit(solution)/shard_map/outputs/pallas_call | solution.py:704

commit v7 on v6

--- a/solution.py
+++ b/solution.py
@@ -70,7 +70,7 @@
         )
 
 
-N_SEMS = 232
+N_SEMS = 272
 
 
 def start(copies):
@@ -137,12 +137,16 @@
         gp = dot(v_twice, jnp.concatenate([gh_m, gh_r], axis=1), ROWS)
         gs = p * (gp - jnp.sum(p * gp, axis=0, keepdims=True))
         highs.append(p_high)
-        left_v += [p_high, p_rest, p_high]
-        right_v += [gh_m, gh_m, gh_r]
+        left_v += [p_high, p_rest]
+        right_v += [
+            jnp.concatenate([gh_m, gh_r], axis=1),
+            jnp.concatenate([gh_m, jnp.zeros_like(gh_m)], axis=1),
+        ]
         grads += list(split(gs))
         right_k += [q * mask] * 2
         left_q += [k * mask] * 2
     gv = dot(jnp.concatenate(left_v, axis=1), jnp.concatenate(right_v, axis=0))
+    gv = gv[:, :128] + gv[:, 128:]
     gk = dot(jnp.concatenate(grads, axis=1), jnp.concatenate(right_k, axis=0))
     gq_t = dot(jnp.concatenate(left_q, axis=0), jnp.concatenate(grads, axis=0), COLS)
     by_head = jnp.concatenate([v * mask for mask in masks], axis=0)
@@ -164,10 +168,11 @@
     sibling = device_at(where, c=1 - c)
     links = Links(send_sems, recv_sems)
     for name, count in (
-        ("quad", 6), ("z0", 7), ("zp", 7), ("z1", 7), ("mid0", 6), ("midp", 6), ("mid1", 6), ("mid2", 6),
+        ("quad", 6), ("z0", 7), ("zp", 7), ("z1", 7), ("midp", 6), ("mid1", 6), ("mid2", 6),
         ("x3", 3),
         ("y3", 3), ("z3", 7),
-        ("bulk", 24), ("across", 32), ("bulk_p", 6), ("across_p", 8), ("core", 4),
+        ("bulk", 24), ("across", 32), ("bulkp", 6), ("acrossp", 8), ("mida", 6), ("bulka", 6), ("acrossa", 8),
+        ("midb", 6), ("bulkb", 6), ("acrossb", 8), ("core", 4),
         ("sum1", 12), ("sum2", 12), ("sum3", 14), ("dir_z", 14), ("dir_mid", 12),
         ("dir_last", 12), ("dir_across", 16),
     ):
@@ -267,18 +272,45 @@
 
     depths = (pl.ds(0, 4), pl.ds(4, 4))
 
-    def middle_p():
+    units = {"a": (0, 0), "b": (1, 0), "p": (0, 4)}
+
+    def unit_lines(unit, p, at):
+        kind, slot = units[unit]
+        if p == 0:
+            return w.at[kind, slot, c, depths[0], :, at // 2, lax.rem(at, 2)]
+        return w.at[kind, slot, c, depths[1], at]
+
+    def unit_middle(unit):
+        kind, slot = units[unit]
         copies = []
         for depth, axis in zip(depths, "yx"):
             for k in SHIFTS[axis]:
-                ref = w.at[0, 4, c, depth, y, xh, xl]
-                copies.append(links.copy("midp", len(copies), ref, ref, peer(axis, k)))
+                ref = w.at[kind, slot, c, depth, y, xh, xl]
+                copies.append(links.copy("mid" + unit, len(copies), ref, ref, peer(axis, k)))
         return copies
 
-    def rank_lines(p, at):
-        if p == 0:
-            return w.at[0, 4, c, depths[0], :, at // 2, lax.rem(at, 2)]
-        return w.at[0, 4, c, depths[1], at]
+    def unit_bulk(unit):
+        copies = []
+        for p, axis in enumerate("xy"):
+            ref = unit_lines(unit, p, where[axis])
+            for k in SHIFTS[axis]:
+                copies.append(links.copy("bulk" + unit, len(copies), ref, ref, peer(axis, k)))
+        return copies
+
+    def unit_across(unit):
+        refs = [unit_lines(unit, 0, x), unit_lines(unit, 1, y)]
+        for p, axis in enumerate("xy"):
+            refs += [unit_lines(unit, p, shifted(where, axis, -k)) for k in SHIFTS[axis]]
+        return [links.copy("across" + unit, i, r, r, sibling) for i, r in enumerate(refs)]
+
+    def open_unit(unit):
+        start(unit_bulk(unit))
+        start(unit_across(unit)[:2])
+
+    def forward_unit(unit):
+        for got, on in zip(unit_bulk(unit), unit_across(unit)[2:]):
+            got.wait_recv()
+            on.start()
 
     def along_x(slot, at):
         return w.at[0, slot, c, :, :, at // 2, lax.rem(at, 2)]
@@ -296,26 +328,12 @@
             copies.append(links.copy("bulk", g * 6 + 3 + i, ref, ref, peer("y", k)))
         return copies
 
-    def bulk_p():
-        copies = []
-        for p, axis in enumerate("xy"):
-            ref = rank_lines(p, where[axis])
-            for k in SHIFTS[axis]:
-                copies.append(links.copy("bulk_p", len(copies), ref, ref, peer(axis, k)))
-        return copies
-
     def across(g):
         refs = [along_x(g, x), along_y(g, y)]
         refs += [along_x(g, shifted(where, "x", -k)) for k in SHIFTS["x"]]
         refs += [along_y(g, shifted(where, "y", -k)) for k in SHIFTS["y"]]
         return [links.copy("across", g * 8 + i, r, r, sibling) for i, r in enumerate(refs)]
 
-    def across_p():
-        refs = [rank_lines(0, x), rank_lines(1, y)]
-        for p, axis in enumerate("xy"):
-            refs += [rank_lines(p, shifted(where, axis, -k)) for k in SHIFTS[axis]]
-        return [links.copy("across_p", i, r, r, sibling) for i, r in enumerate(refs)]
-
     def open_bulk(g):
         start(bulk(g))
         start(across(g)[:2])
@@ -330,21 +348,23 @@
         refs += [w.at[:, 3, c, shifted(where, "z", -k)] for k in SHIFTS["z"]]
         return [links.copy("across", 24 + i, r, r, sibling) for i, r in enumerate(refs)]
 
-    mids = [middle(g) for g in range(GROUPS - 1)]
-    mid_rank = middle_p()
+    mids = {g: middle(g) for g in (1, 2)}
+    unit_mids = {unit: unit_middle(unit) for unit in units}
     received(z_first)
-    start(mids[0])
+    start(unit_mids["a"])
+    start(unit_mids["b"])
     received(z_rank)
-    start(mid_rank)
+    start(unit_mids["p"])
     received(x_last)
     start(y_last)
-    received(mids[0])
-    open_bulk(0)
+    received(unit_mids["a"])
+    open_unit("a")
+    received(unit_mids["b"])
+    open_unit("b")
     received(z_rest)
     start(mids[1])
-    received(mid_rank)
-    start(bulk_p())
-    start(across_p()[:2])
+    received(unit_mids["p"])
+    open_unit("p")
     received(y_last)
     start(z_last)
     start(across_last()[:1])
@@ -363,7 +383,7 @@
                 diagonal[:16], line[i : i + 1, :], F32(0.0)
             ).astype(BF16)
 
-    forward(0)
+    forward_unit("a")
     received(mids[1])
     open_bulk(1)
     start(mids[2])
@@ -383,6 +403,13 @@
             res = dot(src[...], weight(g, low_x, core))
             out[0] = res[:, :128].astype(out.dtype)
             out[1] = res[:, 128:].astype(out.dtype)
+
+    def project_unit(u):
+        for src, low_x, core, out in (
+            (normed, 0, 0, q_s), (normed, 0, 1, k_s), (normed, 1, 0, v_s), (gout_ref, 1, 1, gh_s)
+        ):
+            res = dot(src[...], w[u, 0, core, :, :, :, low_x].reshape(WIDTH, 128))
+            out[u] = res.astype(out.dtype)
 
     def project_rank():
         both = [w[0, 4, core, :, :, :, 0].reshape(WIDTH, 128) for core in range(2)]
@@ -519,7 +546,12 @@
 
         @pl.when(i == 0)
         def _():
-            @pl.when(g < GROUPS - 1)
+            @pl.when(g == 0)
+            def _():
+                received(unit_across("a"))
+                project_unit(0)
+
+            @pl.when((g > 0) & (g < GROUPS - 1))
             def _():
                 received(across(g))
 
@@ -527,12 +559,16 @@
             def _():
                 received(across_last())
 
-            project(g)
+            @pl.when(g > 0)
+            def _():
+                project(g)
 
         @pl.when(i == 1)
         def _():
             @pl.when(g == 0)
             def _():
+                received(unit_across("b"))
+                project_unit(1)
                 received(mids[2])
                 open_bulk(2)
 
@@ -553,9 +589,8 @@
 
             @pl.when(t == 0)
             def _():
-                for got, on in zip(bulk_p(), across_p()[2:]):
-                    got.wait_recv()
-                    on.start()
+                forward_unit("b")
+                forward_unit("p")
 
         gq_t, gk, gv, attended_t = attend_pair(
             q_s[i], k_s[i], v_s[i], gh_s[i], bias, masks, between
@@ -563,7 +598,7 @@
 
         @pl.when(t == 0)
         def _():
-            received(across_p())
+            received(unit_across("p"))
             project_rank()
 
         gq_t = (gq_t * 0.125).astype(BF16)
@@ -615,16 +650,15 @@
     hand_on(1)
     step_of(1)
 
-    sent(quad + z_first + z_rank + z_rest + mid_rank)
-    for copies in mids:
-        sent(copies)
-    sent(bulk_p() + across_p())
+    sent(quad + z_first + z_rank + z_rest + mids[1] + mids[2])
+    for unit in units:
+        sent(unit_mids[unit] + unit_bulk(unit) + unit_across(unit))
 
     @pl.loop(0, GROUPS)
     def _(g):
         sent([core_copy(g)] + sum1(g) + sum2(g))
 
-        @pl.when(g < GROUPS - 1)
+        @pl.when((g > 0) & (g < GROUPS - 1))
         def _():
             sent(bulk(g) + across(g))
 

time: 103 us -> 104 us (level)
  no operation moved by 1% of the time
where the time goes in v7:
time: 104 us
  Pallas kernels  103 us (99%)
    pallas_call x1, Pallas kernels, main(): pl.pallas_call(main_kernel, out_shape=(jax.ShapeDtypeStruct((64, 256), F3...  102 us

profile of v7, /device:TPU:1, one launch (start us, length us, event | category | flops | bytes accessed | tf_op | source)
XLA Modules:
  0.0 103.9 jit_solution(324299452585886283)
XLA Ops:
  0.6 101.6 %galore_step.1 = (f32[64,256]{1,0:T(8,128)}, f32[1,4096]{1,0:T(1,128)}) custom-call(s32[1,4]{1,0:T(1,128)} %len_ref.1, bf16[384,1024]{1,0:T(8,128)(2,1)} %in_ref.1, bf16[384,1024]{1,0:T(8,128)(2,1)} %gout_ref.1, f32[1,1024]{1,0:T(1,128)} %bitcast.1, f32[4,4096]{1,0:T(4,128)} %master_ref.3, bf16[4,256]{1,0:T(4,128)(2,1)} %proj_ref.1, f32[1,4096]{1,0:T(1,128)} %first_ref.3, ...), custom_call_target="tpu_custom_call" | custom-call | tf_op jit(solution)/shard_map/galore_step/pallas_call | solution.py:673
  102.3 1.7 %outputs.1 = (f32[4,4096]{1,0:T(4,128)}, f32[1,4096]{1,0:T(1,128)}, f32[1,4096]{1,0:T(1,128)}) custom-call(f32[64,256]{1,0:T(8,128)} %get-tuple-element.5.step_ref, f32[1,4096]{1,0:T(1,128)} %get-tuple-element.6.low_ref, f32[1,4096]{1,0:T(1,128)} %first_ref.3, f32[1,4096]{1,0:T(1,128)} %second_ref.3, f32[4,4096]{1,0:T(4,128)} %master_ref.3), custom_call_target="tpu_custom_call" | custom-call | tf_op jit(solution)/shard_map/outputs/pallas_call | solution.py:738

commit v8 on v6

--- a/solution.py
+++ b/solution.py
@@ -137,12 +137,16 @@
         gp = dot(v_twice, jnp.concatenate([gh_m, gh_r], axis=1), ROWS)
         gs = p * (gp - jnp.sum(p * gp, axis=0, keepdims=True))
         highs.append(p_high)
-        left_v += [p_high, p_rest, p_high]
-        right_v += [gh_m, gh_m, gh_r]
+        left_v += [p_high, p_rest]
+        right_v += [
+            jnp.concatenate([gh_m, gh_r], axis=1),
+            jnp.concatenate([gh_m, jnp.zeros_like(gh_m)], axis=1),
+        ]
         grads += list(split(gs))
         right_k += [q * mask] * 2
         left_q += [k * mask] * 2
     gv = dot(jnp.concatenate(left_v, axis=1), jnp.concatenate(right_v, axis=0))
+    gv = gv[:, :128] + gv[:, 128:]
     gk = dot(jnp.concatenate(grads, axis=1), jnp.concatenate(right_k, axis=0))
     gq_t = dot(jnp.concatenate(left_q, axis=0), jnp.concatenate(grads, axis=0), COLS)
     by_head = jnp.concatenate([v * mask for mask in masks], axis=0)
@@ -595,8 +599,8 @@
 
     stage_one(GROUPS - 1)
     stage_three(GROUPS - 2)
+    stage_two(GROUPS - 1)
     summed(0)
-    stage_two(GROUPS - 1)
     stage_three(GROUPS - 1)
     start(sum3(1))
     received(dir_z(0))

time: 103 us -> 103 us (level)
  no operation moved by 1% of the time
where the time goes in v8:
time: 103 us
  Pallas kernels  102 us (99%)
    pallas_call x1, Pallas kernels, main(): pl.pallas_call(main_kernel, out_shape=(jax.ShapeDtypeStruct((64, 256), F3...  100 us

profile of v8, /device:TPU:1, one launch (start us, length us, event | category | flops | bytes accessed | tf_op | source)
XLA Modules:
  0.0 102.7 jit_solution(5498454515924073097)
XLA Ops:
  0.6 100.4 %galore_step.1 = (f32[64,256]{1,0:T(8,128)}, f32[1,4096]{1,0:T(1,128)}) custom-call(s32[1,4]{1,0:T(1,128)} %len_ref.1, bf16[384,1024]{1,0:T(8,128)(2,1)} %in_ref.1, bf16[384,1024]{1,0:T(8,128)(2,1)} %gout_ref.1, f32[1,1024]{1,0:T(1,128)} %bitcast.1, f32[4,4096]{1,0:T(4,128)} %master_ref.3, bf16[4,256]{1,0:T(4,128)(2,1)} %proj_ref.1, f32[1,4096]{1,0:T(1,128)} %first_ref.3, ...), custom_call_target="tpu_custom_call" | custom-call | tf_op jit(solution)/shard_map/galore_step/pallas_call | solution.py:643
  101.1 1.7 %outputs.1 = (f32[4,4096]{1,0:T(4,128)}, f32[1,4096]{1,0:T(1,128)}, f32[1,4096]{1,0:T(1,128)}) custom-call(f32[64,256]{1,0:T(8,128)} %get-tuple-element.5.step_ref, f32[1,4096]{1,0:T(1,128)} %get-tuple-element.6.low_ref, f32[1,4096]{1,0:T(1,128)} %first_ref.3, f32[1,4096]{1,0:T(1,128)} %second_ref.3, f32[4,4096]{1,0:T(4,128)} %master_ref.3), custom_call_target="tpu_custom_call" | custom-call | tf_op jit(solution)/shard_map/outputs/pallas_call | solution.py:708

commit v9 on v8

--- a/solution.py
+++ b/solution.py
@@ -540,16 +540,20 @@
                 received(mids[2])
                 open_bulk(2)
 
+            @pl.when(g == 1)
+            def _():
+                forward(2)
+
         def between():
             @pl.when((i == 0) & (g > 0))
             def _():
                 stage_one(g - 1)
 
-            @pl.when((i == 1) & (g < GROUPS - 2))
-            def _():
-                forward(g + 1)
-
-            @pl.when((i == 1) & (g == GROUPS - 2))
+            @pl.when((i == 1) & (g == 0))
+            def _():
+                forward(1)
+
+            @pl.when((i == 0) & (g == GROUPS - 2))
             def _():
                 for got, on in zip(z_last, across_last()[1:]):
                     got.wait_recv()

time: 103 us -> 103 us (level)
  no operation moved by 1% of the time
where the time goes in v9:
time: 103 us
  Pallas kernels  102 us (99%)
    pallas_call x1, Pallas kernels, main(): pl.pallas_call(main_kernel, out_shape=(jax.ShapeDtypeStruct((64, 256), F3...  101 us

profile of v9, /device:TPU:1, one launch (start us, length us, event | category | flops | bytes accessed | tf_op | source)
XLA Modules:
  0.0 103.1 jit_solution(4107085724890118559)
XLA Ops:
  0.6 100.8 %galore_step.1 = (f32[64,256]{1,0:T(8,128)}, f32[1,4096]{1,0:T(1,128)}) custom-call(s32[1,4]{1,0:T(1,128)} %len_ref.1, bf16[384,1024]{1,0:T(8,128)(2,1)} %in_ref.1, bf16[384,1024]{1,0:T(8,128)(2,1)} %gout_ref.1, f32[1,1024]{1,0:T(1,128)} %bitcast.1, f32[4,4096]{1,0:T(4,128)} %master_ref.3, bf16[4,256]{1,0:T(4,128)(2,1)} %proj_ref.1, f32[1,4096]{1,0:T(1,128)} %first_ref.3, ...), custom_call_target="tpu_custom_call" | custom-call | tf_op jit(solution)/shard_map/galore_step/pallas_call | solution.py:647
  101.4 1.7 %outputs.1 = (f32[4,4096]{1,0:T(4,128)}, f32[1,4096]{1,0:T(1,128)}, f32[1,4096]{1,0:T(1,128)}) custom-call(f32[64,256]{1,0:T(8,128)} %get-tuple-element.5.step_ref, f32[1,4096]{1,0:T(1,128)} %get-tuple-element.6.low_ref, f32[1,4096]{1,0:T(1,128)} %first_ref.3, f32[1,4096]{1,0:T(1,128)} %second_ref.3, f32[4,4096]{1,0:T(4,128)} %master_ref.3), custom_call_target="tpu_custom_call" | custom-call | tf_op jit(solution)/shard_map/outputs/pallas_call | solution.py:712

commit v10 on v8

--- a/solution.py
+++ b/solution.py
@@ -367,10 +367,10 @@
                 diagonal[:16], line[i : i + 1, :], F32(0.0)
             ).astype(BF16)
 
-    forward(0)
     received(mids[1])
     open_bulk(1)
     start(mids[2])
+    forward(0)
 
     lane = lax.broadcasted_iota(jnp.int32, (1, 128), 1)
     firsts = (lane < 64).astype(F32).astype(BF16)

time: 103 us -> 103 us (level)
  no operation moved by 1% of the time
where the time goes in v10:
time: 103 us
  Pallas kernels  102 us (99%)
    pallas_call x1, Pallas kernels, main(): pl.pallas_call(main_kernel, out_shape=(jax.ShapeDtypeStruct((64, 256), F3...  100 us

profile of v10, /device:TPU:1, one launch (start us, length us, event | category | flops | bytes accessed | tf_op | source)
XLA Modules:
  0.0 102.8 jit_solution(13383737835515482941)
XLA Ops:
  0.6 100.5 %galore_step.1 = (f32[64,256]{1,0:T(8,128)}, f32[1,4096]{1,0:T(1,128)}) custom-call(s32[1,4]{1,0:T(1,128)} %len_ref.1, bf16[384,1024]{1,0:T(8,128)(2,1)} %in_ref.1, bf16[384,1024]{1,0:T(8,128)(2,1)} %gout_ref.1, f32[1,1024]{1,0:T(1,128)} %bitcast.1, f32[4,4096]{1,0:T(4,128)} %master_ref.3, bf16[4,256]{1,0:T(4,128)(2,1)} %proj_ref.1, f32[1,4096]{1,0:T(1,128)} %first_ref.3, ...), custom_call_target="tpu_custom_call" | custom-call | tf_op jit(solution)/shard_map/galore_step/pallas_call | solution.py:643
  101.1 1.7 %outputs.1 = (f32[4,4096]{1,0:T(4,128)}, f32[1,4096]{1,0:T(1,128)}, f32[1,4096]{1,0:T(1,128)}) custom-call(f32[64,256]{1,0:T(8,128)} %get-tuple-element.5.step_ref, f32[1,4096]{1,0:T(1,128)} %get-tuple-element.6.low_ref, f32[1,4096]{1,0:T(1,128)} %first_ref.3, f32[1,4096]{1,0:T(1,128)} %second_ref.3, f32[4,4096]{1,0:T(4,128)} %master_ref.3), custom_call_target="tpu_custom_call" | custom-call | tf_op jit(solution)/shard_map/outputs/pallas_call | solution.py:708
